TPU v7x, 128 devices: a whole 4x4x4 slice. The times are simulated.
128 devices in a mesh: atm: 16 (over x, z), ocn: 8 (over y, core).
Axes of the slice: x: 4, y: 4, z: 4, core: 2. Of those that a mesh axis runs over, the one named last changes fastest.
Arguments:
- air_member_values: bfloat16 [16, 64, 256, 256], P('ocn', 'atm'), may hold values from -6 to 6
- marine_member_values: bfloat16 [16, 128, 256, 256], P('atm', 'ocn'), may hold values from -6 to 6
- air_neighbour_faces: int32 [64, 4], replicated, may hold values from 0 to 63, as said below
- marine_neighbour_faces: int32 [128, 4], replicated, may hold values from 0 to 127, as said below
- marine_spanned_quarter: int32 [128], replicated, may hold values from 0 to 255, as said below
- water_cell_indicator: int32 [128, 256], P('ocn'), may hold values 0 or 1
- initial_air_filter: bfloat16 [9, 256, 256], replicated, may hold values from -0.125 to 0.125
- initial_filter_offset: float32 [256], replicated, may hold values from -3 to 3
- later_air_filter: bfloat16 [9, 256, 256], replicated, may hold values from -0.125 to 0.125
- later_filter_offset: float32 [256], replicated, may hold values from -3 to 3
- air_to_exchange_matrix: bfloat16 [256, 16], replicated, may hold values from -0.375 to 0.375
- exchange_to_marine_matrix: bfloat16 [16, 256], replicated, may hold values from -1.5 to 1.5
- marine_wide_filter: bfloat16 [49, 256], replicated, may hold values from -0.875 to 0.875
- wide_filter_offset: float32 [256], replicated, may hold values from -3 to 3
- marine_rescale_factor: float32 [256], replicated, may hold values from 0.5 to 1.5
- hidden_entry_matrix: bfloat16 [256, 1024], replicated, may hold values from -0.375 to 0.375
- hidden_entry_offset: float32 [1024], replicated, may hold values from -3 to 3
- hidden_exit_matrix: bfloat16 [1024, 256], replicated, may hold values from -0.1875 to 0.1875
- marine_to_skin_matrix: bfloat16 [256, 16], replicated, may hold values from -0.375 to 0.375
- skin_to_air_matrix: bfloat16 [16, 256], replicated, may hold values from -1.5 to 1.5
Outputs:
- atm_next: bfloat16 [16, 64, 256, 256], P('ocn', 'atm')
- marine_values_advanced: bfloat16 [16, 128, 256, 256], P('atm', 'ocn')
Inputs may be any that keep to these rules, and one draw needn't show every extreme that they name: `air_neighbour_faces`: entry s of row t is the tile beside t on side s (north, south, west, east); the north tile's south tile is t, and the west tile's east tile is t. `marine_neighbour_faces`: entry s of row t is the tile beside t on side s (north, south, west, east); the north tile's south tile is t, and the west tile's east tile is t. `marine_spanned_quarter`: Distinct; for each j exactly one of 2 * j and 2 * j + 1 appears.
All inputs are finite; a program needn't handle non-finite values. No bound on the sum of `water_cell_indicator` on one device may be relied on, other than what follows from the above.
Results may differ from a plain program's by a relative error of at most 0.01.
Values may be sent and summed in bfloat16 or wider, within the bound.
A program may use at most 128 MiB of HBM per device.

v0:
```python
import math

import jax
import jax.numpy as jnp
from jax import lax
from jax.sharding import PartitionSpec as P


def edge_rims(state, width):
    upper = state[..., :width, :, :]
    lower = state[..., -width:, :, :]
    left_side = jnp.swapaxes(state[..., :, :width, :], -2, -3)
    right_side = jnp.swapaxes(state[..., :, -width:, :], -2, -3)
    rims = jnp.stack([upper, lower, left_side, right_side], axis=-4)
    return rims.reshape(state.shape[:-3] + (-1,))


def assemble(state, whole, tile_rows, width):
    side = state.shape[-2]
    chans = state.shape[-1]
    pieces = whole.reshape(whole.shape[:2] + (4, width, side, chans))
    north = jnp.take(pieces[:, :, 1], tile_rows[:, 0], axis=1)
    south = jnp.take(pieces[:, :, 0], tile_rows[:, 1], axis=1)
    west = jnp.swapaxes(jnp.take(pieces[:, :, 3], tile_rows[:, 2], axis=1), -2, -3)
    east = jnp.swapaxes(jnp.take(pieces[:, :, 2], tile_rows[:, 3], axis=1), -2, -3)
    middle = jnp.concatenate([west, state, east], axis=-2)
    blank = jnp.zeros(north.shape[:-3] + (width, width, chans), state.dtype)
    upper = jnp.concatenate([blank, north, blank], axis=-2)
    lower = jnp.concatenate([blank, south, blank], axis=-2)
    return jnp.concatenate([upper, middle, lower], axis=-3)


def atm_layer(state, air_neighbour_faces, kernel, bias):
    tiles_here = state.shape[1]
    side = state.shape[2]
    whole = lax.all_gather(edge_rims(state, 1), "atm", axis=1, tiled=True)
    tile_rows = lax.dynamic_slice_in_dim(
        air_neighbour_faces, lax.axis_index("atm") * tiles_here, tiles_here, 0
    )
    padded = assemble(state, whole, tile_rows, 1)
    total = jnp.zeros(state.shape, jnp.float32)
    for offset in range(9):
        row_shift, col_shift = divmod(offset, 3)
        window = padded[:, :, row_shift : row_shift + side, col_shift : col_shift + side, :]
        total = total + jnp.einsum(
            "mtpqc,cd->mtpqd", window, kernel[offset], preferred_element_type=jnp.float32
        )
    total = total + bias
    result = state.astype(jnp.float32) + jax.nn.gelu(total)
    return result.astype(jnp.bfloat16)


def on_device(
    air_member_values,
    marine_member_values,
    air_neighbour_faces,
    marine_neighbour_faces,
    marine_spanned_quarter,
    water_cell_indicator,
    initial_air_filter,
    initial_filter_offset,
    later_air_filter,
    later_filter_offset,
    air_to_exchange_matrix,
    exchange_to_marine_matrix,
    marine_wide_filter,
    wide_filter_offset,
    marine_rescale_factor,
    hidden_entry_matrix,
    hidden_entry_offset,
    hidden_exit_matrix,
    marine_to_skin_matrix,
    skin_to_air_matrix,
):
    mem_here, atm_tiles, cells, chans = air_member_values.shape
    ocean_tiles = marine_member_values.shape[1]
    side = math.isqrt(cells)
    half_side = side // 2
    couple = air_to_exchange_matrix.shape[1]
    tiles_total = air_neighbour_faces.shape[0]
    quad_cells = couple * half_side * half_side
    state = air_member_values.reshape(mem_here, atm_tiles, side, side, chans)
    first = atm_layer(state, air_neighbour_faces, initial_air_filter, initial_filter_offset)
    split_first = first.reshape(mem_here, atm_tiles, 2, half_side, 2, half_side, chans)
    flux = jnp.einsum(
        "mtaybxc,cf->mtabyxf",
        split_first,
        air_to_exchange_matrix,
        preferred_element_type=jnp.float32,
    ).astype(jnp.bfloat16)
    flux = flux.reshape(mem_here, atm_tiles * 4, quad_cells)
    every_member = lax.all_gather(flux, "ocn", axis=0, tiled=True)
    spread = lax.all_to_all(every_member, "atm", split_axis=0, concat_axis=1, tiled=True)
    local_ids = lax.dynamic_slice_in_dim(
        marine_spanned_quarter, lax.axis_index("ocn") * ocean_tiles, ocean_tiles, 0
    )
    chosen = jnp.take(spread, local_ids, axis=1)
    coarse_in = chosen.reshape(1, ocean_tiles, half_side, half_side, couple)
    forcing = jnp.einsum(
        "styxf,fc->styxc", coarse_in, exchange_to_marine_matrix, preferred_element_type=jnp.float32
    )
    forcing = jnp.repeat(jnp.repeat(forcing, 2, axis=3), 2, axis=2)
    sea = water_cell_indicator.reshape(1, ocean_tiles, side, side, 1).astype(jnp.float32)
    ocean = marine_member_values.reshape(1, ocean_tiles, side, side, chans)
    forced = ocean.astype(jnp.float32) + forcing
    masked = (forced * sea).astype(jnp.bfloat16)
    ocean_whole = lax.all_gather(edge_rims(masked, 3), "ocn", axis=1, tiled=True)
    ocean_table = lax.dynamic_slice_in_dim(
        marine_neighbour_faces, lax.axis_index("ocn") * ocean_tiles, ocean_tiles, 0
    )
    padded = assemble(masked, ocean_whole, ocean_table, 3)
    depth = jnp.zeros(forced.shape, jnp.float32) + wide_filter_offset
    for offset in range(49):
        row_shift, col_shift = divmod(offset, 7)
        window = padded[:, :, row_shift : row_shift + side, col_shift : col_shift + side, :]
        depth = depth + window.astype(jnp.float32) * marine_wide_filter[offset].astype(jnp.float32)
    center = jnp.mean(depth, axis=4, keepdims=True)
    variance = jnp.mean((depth - center) ** 2, axis=4, keepdims=True)
    normed = ((depth - center) * lax.rsqrt(variance + 1e-06) * marine_rescale_factor).astype(
        jnp.bfloat16
    )
    inner = (
        jnp.einsum(
            "stpqc,ch->stpqh", normed, hidden_entry_matrix, preferred_element_type=jnp.float32
        )
        + hidden_entry_offset
    )
    inner = jax.nn.gelu(inner).astype(jnp.bfloat16)
    outer = jnp.einsum(
        "stpqh,hc->stpqc", inner, hidden_exit_matrix, preferred_element_type=jnp.float32
    )
    marine_values_advanced = (sea * (forced + outer)).astype(jnp.bfloat16)
    skin_quantities = jnp.einsum(
        "stpqc,cf->stpqf",
        marine_values_advanced,
        marine_to_skin_matrix,
        preferred_element_type=jnp.float32,
    ).astype(jnp.bfloat16)
    blocks = skin_quantities.astype(jnp.float32).reshape(
        1, ocean_tiles, half_side, 2, half_side, 2, couple
    )
    coarse = (
        (jnp.sum(blocks, axis=(3, 5)) * 0.25)
        .astype(jnp.bfloat16)
        .reshape(1, ocean_tiles, quad_cells)
    )
    scattered = (
        jnp.zeros((1, 4 * tiles_total, quad_cells), jnp.float32)
        .at[:, local_ids]
        .set(coarse.astype(jnp.float32))
    )
    placed = lax.psum(scattered.astype(jnp.bfloat16), "ocn")
    returned = lax.all_to_all(placed, "atm", split_axis=1, concat_axis=0, tiled=True)
    mine = lax.dynamic_slice_in_dim(returned, lax.axis_index("ocn") * mem_here, mem_here, 0)
    mine = mine.reshape(mem_here, atm_tiles, 2, 2, half_side, half_side, couple)
    back = jnp.einsum(
        "mtabyxf,fc->mtaybxc", mine, skin_to_air_matrix, preferred_element_type=jnp.float32
    )
    back = back.reshape(mem_here, atm_tiles, side, side, chans)
    second = (first.astype(jnp.float32) + back).astype(jnp.bfloat16)
    atm_next = atm_layer(second, air_neighbour_faces, later_air_filter, later_filter_offset)
    return (
        atm_next.reshape(air_member_values.shape),
        marine_values_advanced.reshape(marine_member_values.shape),
    )


def solution(mesh):
    in_specs = (
        P("ocn", "atm", None, None),
        P("atm", "ocn", None, None),
        P(),
        P(),
        P(),
        P("ocn", None),
        P(),
        P(),
        P(),
        P(),
        P(),
        P(),
        P(),
        P(),
        P(),
        P(),
        P(),
        P(),
        P(),
        P(),
    )
    out_specs = (P("ocn", "atm", None, None), P("atm", "ocn", None, None))
    return jax.shard_map(
        on_device, mesh=mesh, in_specs=in_specs, out_specs=out_specs, check_vma=False
    )
```

profile of v0, /device:TPU:1, one launch (start us, length us, event | category | flops | bytes accessed | tf_op | source)
XLA Modules:
  0.0 526.8 jit_solution(9390946075361585527)
XLA Ops:
  7.2 1.6 fusion.141
  11.5 2.7 fusion.98
  14.1 51.5 %all-gather.4.cloned.1.call-done = bf16[2,64,16384]{2,0,1:T(2,128)(2,1)} async-done(((bf16[2,4,16384]{2,0,1:T(2,128)(2,1)}), bf16[2,64,16384]{2,0,1:T(2,128)(2,1)}) %all-gather.4.cloned.1.call-update) | async-done | bytes 4194320 | tf_op jit(solution)/shard_map/all_gather | solution.py:36
  65.6 7.6 %reshape.1010 = bf16[2,64,4,1,16,256]{5,4,2,0,1,3:T(8,128)(2,1)} reshape(bf16[2,64,16384]{2,0,1:T(2,128)(2,1)} %all-gather.4.cloned.1.call-done) | data formatting | bytes 8388608 | tf_op jit(solution)/shard_map/reshape | solution.py:21
  73.2 4.1 fusion.139
  77.3 1.1 copy.343
  78.4 1.8 gather_fusion.2
  80.4 2.3 copy.342
  82.7 1.8 gather_fusion.3
  84.7 2.3 copy.344
  88.0 1.8 gather_fusion.1
  89.9 1.8 gather_fusion.4
  91.7 2.4 fusion.40
  94.1 1.4 fusion.59
  98.9 1.8 fusion.23
  103.0 15.1 %all_gather.13 = bf16[16,16,1024]{2,1,0:T(8,128)(2,1)} all-gather(bf16[2,16,1024]{2,1,0:T(8,128)(2,1)S(1)} %reshape.713), channel_id=1, replica_groups=mesh['atm'=16,'ocn'=8] {'ocn'}, dimensions={0}, use_global_device_ids=true | all-gather | bytes 589824 | tf_op jit(solution)/shard_map/all_gather | solution.py:92
  118.0 5.0 all-to-all-start
  123.3 2.5 convert_element_type.936
  126.1 7.1 %all-to-all-done = bf16[16,16,1024]{2,1,0:T(8,128)(2,1)S(1)} async-done(((bf16[16,16,1024]{2,1,0:T(8,128)(2,1)}), bf16[16,16,1024]{2,1,0:T(8,128)(2,1)S(1)}, u32[]{:S(2)}, u32[]{:S(2)}) %all-to-all-start) | async-done | bytes 524320 | tf_op jit(solution)/shard_map/all_to_all | solution.py:93
  134.4 2.5 broadcast_in_dim.48
  136.8 2.7 broadcast_in_dim.49
  140.1 3.2 copy-done.2
  143.2 4.7 fusion.9
  148.7 1.3 pad_maximum_fusion.11
  150.0 2.8 reshape.714
  156.9 62.6 %all-gather.6.cloned.1.call-done = bf16[1,128,49152]{2,1,0:T(8,128)(2,1)} async-done(((bf16[1,16,49152]{2,1,0:T(8,128)(2,1)}), bf16[1,128,49152]{2,1,0:T(8,128)(2,1)}) %all-gather.6.cloned.1.call-update) | async-done | bytes 12582928 | tf_op jit(solution)/shard_map/all_gather | solution.py:107
  219.6 16.6 %copy.221 = bf16[1,128,49152]{1,2,0:T(8,128)(2,1)} copy(bf16[1,128,49152]{2,1,0:T(8,128)(2,1)} %all-gather.6.cloned.1.call-done) | data formatting | bytes 25165824 | tf_op jit(solution)/shard_map/all_gather | solution.py:107
  236.1 9.7 %fusion.137 = (bf16[1,128,1,3,16,256]{1,5,4,3,2,0:T(8,128)(2,1)}, bf16[1,128,1,3,16,256]{1,5,4,3,2,0:T(8,128)(2,1)}, bf16[1,128,1,3,16,256]{1,5,4,3,2,0:T(8,128)(2,1)}, bf16[1,128,1,3,16,256]{1,5,4,3,2,0:T(8,128)(2,1)}) fusion(bf16[1,128,4,3,16,256]{1,5,4,3,2,0:T(8,128)(2,1)} %bitcast.429), kind=kLoop, calls=%fused_computation.310 | loop fusion | bytes 25165824 | tf_op jit(solution)/shard_map/slice | solution.py:22
  245.8 4.9 copy.299
  250.7 4.9 copy.296
  255.6 2.5 gather_fusion.8
  258.8 2.6 gather_fusion.5
  262.8 1.1 copy.225
  263.9 1.1 copy.227
  265.1 5.0 copy.297
  270.1 4.9 copy.298
  275.0 2.6 gather_fusion.6
  278.3 2.6 gather_fusion.7
  282.0 4.3 maximum_maximum_fusion
  286.7 35.7 %fusion.136 = (f32[16,16,16]{1,2,0:T(8,128)S(1)}, f32[1,16,16,16,256]{4,2,3,1,0:T(8,128)S(1)}) fusion(f32[256]{0:T(256)S(1)} %bitcast.473, bf16[1,16,19,22,256]{4,2,3,1,0:T(8,128)(2,1)S(1)} %get-tuple-element.37, f32[256]{0:T(256)S(1)} %bitcast.474, f32[256]{0:T(256)S(1)} %bitcast.495, f32[256]{0:T(256)S(1)} %bitcast.496, f32[256]{0:T(256)S(1)} %bitcast.497, ...), kind=kLoop, calls=%fused_computation.309 | loop fusion | flops 161476608 | bytes 95225856 | tf_op jit(solution)/shard_map/reduce_sum | solution.py:117
  322.4 1.4 multiply_reduce_fusion
  323.8 2.3 fusion.33
  326.1 10.3 %multiply_convert_fusion = bf16[16,16,16,256]{3,2,1,0:T(8,128)(2,1)S(1)} fusion(f32[16,16,16,256]{3,2,1,0:T(8,128)} %bitcast.437, f32[16,16,16,256]{3,2,1,0:T(8,128)} %bitcast.440, f32[16,16,16]{2,1,0:T(8,128)S(1)} %convert_element_type.770, f32[1024]{0:T(1024)S(1)} %copy-done.78, bf16[16,16,16,256]{3,1,2,0:T(8,128)(2,1)} %fusion.33, ...), kind=kOutput, calls=%fused_computation.28 | convolution fusion | flops 4341104640 | bytes 13651968 | tf_op jit(solution)/shard_map/stpqh,hc->stpqc/dot_general | solution.py:129
  337.1 2.1 convert_reduce_fusion
  341.4 58.8 %all-reduce.2.cloned.1.call-done = bf16[1,256,1024]{2,1,0:T(8,128)(2,1)} async-done(((bf16[1,256,1024]{2,1,0:T(8,128)(2,1)}), bf16[1,256,1024]{2,1,0:T(8,128)(2,1)}) %all-reduce.2.cloned.1.call-update) | async-done | bytes 524304 | tf_op jit(solution)/shard_map/psum | solution.py:152
  400.3 1.9 copy.347
  402.7 3.7 reduce.3
  406.4 1.2 reshape.1015
  407.6 6.7 %all-to-all-start.1 = ((bf16[16,2,8192]{2,1,0:T(2,128)(2,1)}), bf16[16,2,8192]{2,1,0:T(2,128)(2,1)S(1)}, u32[]{:S(2)}, u32[]{:S(2)}) async-start(bf16[16,2,8192]{2,1,0:T(2,128)(2,1)} %reshape.1015), calls=%async_computation.1 | async-start | bytes 1048576 | tf_op jit(solution)/shard_map/all_to_all | solution.py:153
  414.3 8.9 %all-to-all-done.1 = bf16[16,2,8192]{2,1,0:T(2,128)(2,1)S(1)} async-done(((bf16[16,2,8192]{2,1,0:T(2,128)(2,1)}), bf16[16,2,8192]{2,1,0:T(2,128)(2,1)S(1)}, u32[]{:S(2)}, u32[]{:S(2)}) %all-to-all-start.1) | async-done | bytes 524320 | tf_op jit(solution)/shard_map/all_to_all | solution.py:153
  427.3 2.6 fusion.88
  430.0 50.3 %all-gather.8.cloned.1.call-done = bf16[2,64,16384]{2,0,1:T(2,128)(2,1)} async-done(((bf16[2,4,16384]{2,0,1:T(2,128)(2,1)}), bf16[2,64,16384]{2,0,1:T(2,128)(2,1)}) %all-gather.8.cloned.1.call-update) | async-done | bytes 4194320 | tf_op jit(solution)/shard_map/all_gather | solution.py:36
  480.3 7.6 %reshape.1012 = bf16[2,64,4,1,16,256]{5,4,2,0,1,3:T(8,128)(2,1)} reshape(bf16[2,64,16384]{2,0,1:T(2,128)(2,1)} %all-gather.8.cloned.1.call-done) | data formatting | bytes 8388608 | tf_op jit(solution)/shard_map/reshape | solution.py:21
  487.9 4.0 fusion.138
  491.9 1.1 copy.339
  492.9 1.9 gather_fusion.10
  495.1 2.8 fusion.50
  498.9 1.9 gather_fusion.11
  501.1 2.9 fusion.48
  505.0 1.8 gather_fusion.12
  507.9 1.8 gather_fusion.9
  509.8 2.4 fusion.41
  512.2 1.4 fusion.44
  517.3 2.8 fusion.32
  (252 shorter events, 35.5 us)
Async XLA Ops:
  7.2 318.9 %copy-start = (bf16[1024,256]{1,0:T(8,128)(2,1)S(1)}, bf16[1024,256]{1,0:T(8,128)(2,1)}, u32[]{:S(2)}) copy-start(bf16[1024,256]{1,0:T(8,128)(2,1)} %param.41) | copy-start | bytes 1572868
  7.2 4.3 copy-start.1
  7.2 58.5 %all-gather.4.cloned.1.call-start = ((), (), s32[]{:S(2)}) async-start(), calls=%async_computation.2 | async-start | bytes 4456448 | tf_op jit(solution)/shard_map/all_gather | solution.py:36
  11.4 68.8 %copy-start.30 = (pred[4]{0:T(512)(128)(4,1)}, pred[4]{0:T(512)(128)(4,1)S(1)}, u32[]{:S(2)}) copy-start(pred[4]{0:T(512)(128)(4,1)S(1)} %get-tuple-element.115) | copy-start | bytes 16
  11.4 73.1 %copy-start.28 = (pred[4]{0:T(512)(128)(4,1)}, pred[4]{0:T(512)(128)(4,1)S(1)}, u32[]{:S(2)}) copy-start(pred[4]{0:T(512)(128)(4,1)S(1)} %get-tuple-element.113) | copy-start | bytes 16
  11.4 78.4 %copy-start.24 = (pred[4]{0:T(512)(128)(4,1)}, pred[4]{0:T(512)(128)(4,1)S(1)}, u32[]{:S(2)}) copy-start(pred[4]{0:T(512)(128)(4,1)S(1)} %get-tuple-element.16) | copy-start | bytes 16
  11.4 80.2 %copy-start.26 = (pred[4]{0:T(512)(128)(4,1)}, pred[4]{0:T(512)(128)(4,1)S(1)}, u32[]{:S(2)}) copy-start(pred[4]{0:T(512)(128)(4,1)S(1)} %get-tuple-element.111) | copy-start | bytes 16
  11.4 67.0 %copy-start.23 = (s32[1024]{0:T(1024)}, s32[1024]{0:T(1024)S(1)}, u32[]{:S(2)}) copy-start(s32[1024]{0:T(1024)S(1)} %get-tuple-element.121) | copy-start | bytes 12292
  11.5 71.2 %copy-start.22 = (s32[1024]{0:T(1024)}, s32[1024]{0:T(1024)S(1)}, u32[]{:S(2)}) copy-start(s32[1024]{0:T(1024)S(1)} %get-tuple-element.120) | copy-start | bytes 12292
  100.7 22.5 %copy-start.12 = (bf16[1,16,256,256]{3,2,1,0:T(8,128)(2,1)S(1)}, bf16[1,16,256,256]{3,2,1,0:T(8,128)(2,1)}, u32[]{:S(2)}) copy-start(bf16[1,16,256,256]{3,2,1,0:T(8,128)(2,1)} %param.25) | copy-start | bytes 6291460
  118.0 15.1 %all-to-all-start = ((bf16[16,16,1024]{2,1,0:T(8,128)(2,1)}), bf16[16,16,1024]{2,1,0:T(8,128)(2,1)S(1)}, u32[]{:S(2)}, u32[]{:S(2)}) async-start(bf16[16,16,1024]{2,1,0:T(8,128)(2,1)} %all_gather.13), calls=%async_computation | async-start | bytes 1048576 | tf_op jit(solution)/shard_map/all_to_all | solution.py:93
  123.0 96.6 %all-gather.6.cloned.1.call-start = ((), (), s32[]{:S(2)}) async-start(), calls=%async_computation.3 | async-start | bytes 14155776 | tf_op jit(solution)/shard_map/all_gather | solution.py:107
  123.3 10.7 %copy-start.19 = (bf16[16,256]{1,0:T(8,128)(2,1)S(1)}, bf16[16,256]{1,0:T(8,128)(2,1)}, u32[]{:S(2)}) copy-start(bf16[16,256]{1,0:T(8,128)(2,1)} %param.35) | copy-start | bytes 24580
  126.1 7.1 %copy-start.74 = (s32[16]{0:T(128)}, s32[16]{0:T(128)S(1)}, u32[]{:S(2)}) copy-start(s32[16]{0:T(128)S(1)} %get-tuple-element.15) | copy-start | bytes 196
  140.1 7.8 %copy-start.3 = (f32[16,8,2,16,256]{4,3,2,1,0:T(8,128)}, f32[16,8,2,16,256]{4,3,2,1,0:T(8,128)S(1)}, u32[]{:S(2)}) copy-start(f32[16,8,2,16,256]{4,3,2,1,0:T(8,128)S(1)} %broadcast_in_dim.50) | copy-start | bytes 12582916
  150.0 4.9 copy-start.16
  152.9 247.4 %all-reduce.2.cloned.1.call-start = ((), (), s32[]{:S(2)}) async-start(), calls=%async_computation.4 | async-start | bytes 1048576 | tf_op jit(solution)/shard_map/psum | solution.py:152
  281.6 4.7 copy-start.34
  281.6 4.7 copy-start.35
  281.6 4.7 copy-start.36
  281.6 4.7 copy-start.37
  281.7 4.7 copy-start.38
  281.7 4.7 copy-start.39
  281.7 4.7 copy-start.40
  281.7 4.7 copy-start.41
  281.7 4.7 copy-start.42
  281.7 4.7 copy-start.43
  281.7 4.7 copy-start.44
  281.7 4.7 copy-start.45
  281.7 4.7 copy-start.46
  281.7 4.7 copy-start.47
  281.8 4.7 copy-start.48
  281.8 4.7 copy-start.49
  281.8 4.7 copy-start.50
  281.8 4.7 copy-start.51
  281.8 4.7 copy-start.52
  281.8 4.7 copy-start.53
  281.8 4.7 copy-start.54
  281.8 4.7 copy-start.55
  281.8 4.7 copy-start.56
  281.8 4.7 copy-start.57
  281.9 4.7 copy-start.58
  281.9 4.7 copy-start.59
  281.9 4.7 copy-start.60
  281.9 4.7 copy-start.61
  281.9 4.7 copy-start.62
  281.9 4.7 copy-start.63
  281.9 4.7 copy-start.64
  281.9 4.7 copy-start.65
  281.9 4.7 copy-start.66
  281.9 4.7 copy-start.67
  282.0 4.7 copy-start.68
  282.0 4.7 copy-start.69
  282.0 4.7 copy-start.70
  282.0 4.7 copy-start.71
  282.0 4.7 copy-start.72
  326.1 10.3 %copy-start.20 = (bf16[256,16]{0,1:T(8,128)(2,1)S(1)}, bf16[256,16]{0,1:T(8,128)(2,1)}, u32[]{:S(2)}) copy-start(bf16[256,16]{0,1:T(8,128)(2,1)} %param.42) | copy-start | bytes 24580
  406.4 18.1 %copy-start.21 = (bf16[16,256]{1,0:T(8,128)(2,1)S(1)}, bf16[16,256]{1,0:T(8,128)(2,1)}, u32[]{:S(2)}) copy-start(bf16[16,256]{1,0:T(8,128)(2,1)} %param.43) | copy-start | bytes 24580
  407.6 15.6 %all-to-all-start.1 = ((bf16[16,2,8192]{2,1,0:T(2,128)(2,1)}), bf16[16,2,8192]{2,1,0:T(2,128)(2,1)S(1)}, u32[]{:S(2)}, u32[]{:S(2)}) async-start(bf16[16,2,8192]{2,1,0:T(2,128)(2,1)} %reshape.1015), calls=%async_computation.1 | async-start | bytes 1048576 | tf_op jit(solution)/shard_map/all_to_all | solution.py:153
  414.3 66.0 %all-gather.8.cloned.1.call-start = ((), (), s32[]{:S(2)}) async-start(), calls=%async_computation.5 | async-start | bytes 4456448 | tf_op jit(solution)/shard_map/all_gather | solution.py:36
  487.9 7.0 %copy-start.31 = (pred[4]{0:T(512)(128)(4,1)S(1)}, pred[4]{0:T(512)(128)(4,1)}, u32[]{:S(2)}) copy-start(pred[4]{0:T(512)(128)(4,1)} %copy-done.30) | copy-start | bytes 16
  492.9 7.9 %copy-start.29 = (pred[4]{0:T(512)(128)(4,1)S(1)}, pred[4]{0:T(512)(128)(4,1)}, u32[]{:S(2)}) copy-start(pred[4]{0:T(512)(128)(4,1)} %copy-done.28) | copy-start | bytes 16
  498.9 7.9 %copy-start.27 = (pred[4]{0:T(512)(128)(4,1)S(1)}, pred[4]{0:T(512)(128)(4,1)}, u32[]{:S(2)}) copy-start(pred[4]{0:T(512)(128)(4,1)} %copy-done.26) | copy-start | bytes 16
  504.0 5.8 %copy-start.25 = (pred[4]{0:T(512)(128)(4,1)S(1)}, pred[4]{0:T(512)(128)(4,1)}, u32[]{:S(2)}) copy-start(pred[4]{0:T(512)(128)(4,1)} %copy-done.24) | copy-start | bytes 16
  (21 other events, 52.3 us)
Sparse Core Ops, SparseCore 0:
  10.7 54.8 all-gather.3
  153.0 66.5 all-gather.5
  341.6 58.6 all-reduce.1
  427.4 52.8 all-gather.7
where the time goes:
time: 537 us; the launch traced here: 527 us
  waiting for transfers between devices  239 us (45%)
  local copies, waits for them, and re-layouts  138 us (26%)
  other arithmetic  71.9 us (13%)
  matrix products  35 us (7%)
  between operations  15.6 us (3%)
  blocking collectives  15.1 us (3%)
  starting transfers between devices  12.2 us (2%)
    all_gather x2, waiting for transfers between devices, atm_layer(): whole = lax.all_gather(edge_rims(state, 1), 'atm', axis=1, tiled=True)  102 us
    all_gather x1, waiting for transfers between devices, on_device(): lax.all_gather(edge_rims(masked, 3), 'ocn', axis=1, tiled=True)  62.6 us
    psum x1, waiting for transfers between devices, on_device(): placed = lax.psum(scattered.astype(jnp.bfloat16), 'ocn')  58.8 us
    unnamed x177, local copies, waits for them, and re-layouts  40.8 us
    reduce_sum x1, other arithmetic, on_device(): center = jnp.mean(depth, axis=4, keepdims=True)  35.7 us
    dot_general x18, matrix products, atm_layer(): jnp.einsum('mtpqc,cd->mtpqd', window, kernel[offset], preferred_element_t...  22.9 us
    slice x3, local copies, waits for them, and re-layouts, assemble(): north = jnp.take(pieces[:, :, 1], tile_rows[:, 0], axis=1)  17.8 us
    all_gather x1, local copies, waits for them, and re-layouts, on_device(): lax.all_gather(edge_rims(masked, 3), 'ocn', axis=1, tiled=True)  16.6 us
  transfers between devices with their start and end apart: 6, of which 6 were waited for; matrix products, arithmetic and copies ran while one was open for 2% of the time, Pallas kernels for 0%

commit v1 on v0

v1 whole, which is shorter than its diff:
```python
import functools

import jax
import jax.numpy as jnp
import numpy as np
from jax import lax
from jax.experimental import pallas as pl
from jax.experimental.pallas import tpu as pltpu
from jax.sharding import PartitionSpec as P

BF = jnp.bfloat16
F32 = jnp.float32
MESH = pl.DeviceIdType.MESH
VMEM = pl.BlockSpec(memory_space=pltpu.VMEM)
SMEM = pl.BlockSpec(memory_space=pltpu.SMEM)
HBM = pl.BlockSpec(memory_space=pl.ANY)
C0 = 0.7978845608028654
C1 = C0 * 0.044715


def gelu(x):
    half = 0.5 * x
    return half + half * jnp.tanh(x * (C0 + C1 * (x * x)))


def dot(a, b):
    return jnp.dot(a, b, preferred_element_type=F32)


def dot_t(a, b):
    return lax.dot_general(a, b, (((0,), (0,)), ((), ())), preferred_element_type=F32)


def quarter_tables():
    split = np.zeros((256, 256), np.float32)
    join = np.zeros((256, 256), np.float32)
    for r in range(16):
        for q in range(16):
            a, b = r // 8, q // 8
            cell = (r % 8) * 8 + q % 8
            split[r * 16 + q, b * 128 + a * 64 + cell] = 1
            join[a * 128 + b * 64 + cell, r * 16 + q] = 1
    strip = np.zeros((4, 256, 128), np.float32)
    for c in range(16):
        for side, cell in enumerate((240 + c, c, c * 16 + 15, c * 16)):
            strip[side, :, side * 16 + c] = join[:, cell]
    up = np.zeros((128, 256), np.float32)
    for r in range(16):
        for q in range(16):
            up[(r // 2) * 8 + q // 2, r * 16 + q] = 1
    pick = np.zeros((4, 256, 256), np.float32)
    for j in range(3):
        for c in range(16):
            cells = ((13 + j) * 16 + c, j * 16 + c, c * 16 + 13 + j, c * 16 + j)
            for side, cell in enumerate(cells):
                pick[side, cell, side * 64 + j * 16 + c] = 1
    up_rim = np.einsum("qc,scd->sqd", up, pick)
    mean = np.zeros((2, 256, 128), np.float32)
    for r in range(16):
        for q in range(16):
            for h in range(2):
                mean[h, r * 16 + q, h * 64 + (r // 2) * 8 + q // 2] = 0.25
    cast = lambda v: jnp.asarray(v, BF)
    return (
        cast(split),
        cast(join),
        cast(strip.reshape(1024, 128)),
        cast(up),
        cast(up_rim.reshape(512, 256)),
        cast(pick.reshape(1024, 256)),
        cast(mean),
    )


def rims_kernel(marine, sea, rims, square):
    share = jnp.full((16, 256), 0.0625, BF)

    @pl.loop(0, 16)
    def _(t):
        row = jnp.broadcast_to(sea[pl.ds(t, 1), :].astype(F32), (16, 256)).astype(BF)
        wet = marine[t].astype(F32) * dot_t(row, share)
        rims[t, 0:48] = wet[0:48].astype(BF)
        rims[t, 48:96] = wet[208:256].astype(BF)
        square[...] = wet.reshape(16, 16, 256)
        for j in range(3):
            rims[t, 96 + 16 * j : 112 + 16 * j] = square[:, j, :].astype(BF)
            rims[t, 144 + 16 * j : 160 + 16 * j] = square[:, 13 + j, :].astype(BF)


def coordinates():
    a = lax.axis_index("atm")
    o = lax.axis_index("ocn")
    return a, o, lax.div(a, 4), lax.rem(a, 4)


def axis_partner(mm, phase, d):
    a, o, x, z = coordinates()
    if (mm + phase) % 2 == 0:
        place = lax.rem(z + d, 4)
        return (x * 4 + place, o), place
    place = lax.rem(x + d, 4)
    return (place * 4 + z, o), place


def rim_exchange(rd, tiles, nbr, square, g1, st, r2, send, recv):
    a, o, x, z = coordinates()

    def first_copy(mm, d):
        target, _ = axis_partner(mm, 0, d)
        _, here = axis_partner(mm, 0, 0)
        part = g1[rd][mm].at[here]
        return pltpu.make_async_remote_copy(
            src_ref=part, dst_ref=part, send_sem=send.at[rd, 0, mm, d - 1],
            recv_sem=recv.at[rd, 0, mm, d - 1], device_id=target, device_id_type=MESH)

    def second_copy(mm, d):
        target, _ = axis_partner(mm, 1, d)
        _, here = axis_partner(mm, 1, 0)
        return pltpu.make_async_remote_copy(
            src_ref=st.at[rd, mm, d - 1], dst_ref=r2[rd][mm].at[here],
            send_sem=send.at[rd, 1, mm, d - 1], recv_sem=recv.at[rd, 1, mm, d - 1],
            device_id=target, device_id_type=MESH)

    for mm in range(2):
        _, here = axis_partner(mm, 0, 0)

        @pl.loop(0, 4)
        def _(k):
            tile = tiles[mm, k]
            square[...] = tile.astype(F32).reshape(16, 16, 256)
            g1[rd][mm][here, k * 4] = tile[0:16]
            g1[rd][mm][here, k * 4 + 1] = tile[240:256]
            g1[rd][mm][here, k * 4 + 2] = square[:, 0, :].astype(BF)
            g1[rd][mm][here, k * 4 + 3] = square[:, 15, :].astype(BF)

        for d in (1, 3, 2):
            first_copy(mm, d).start()
    for mm in range(2):
        for d in (1, 2, 3):
            first_copy(mm, d).wait_recv()
        for d in (2, 1, 3, 0):
            (dest, _), place = axis_partner(mm, 1, d)

            @pl.loop(0, 16)
            def _(slot):
                n = nbr[dest * 16 + slot]
                owner = lax.div(n, 4)
                from_place = lax.rem(owner, 4) if mm == 0 else lax.div(owner, 4)
                side = lax.rem(slot, 4)
                kind = side + 1 - 2 * lax.rem(side, 2)
                strip = g1[rd][mm][from_place, lax.rem(n, 4) * 4 + kind]
                if d == 0:
                    r2[rd][mm][place, slot] = strip
                else:
                    st[rd, mm, d - 1, slot] = strip

            if d > 0:
                second_copy(mm, d).start()

    def finish():
        for mm in range(2):
            for d in (1, 2, 3):
                second_copy(mm, d).wait_recv()
        for mm in range(2):
            for d in (1, 2, 3):
                first_copy(mm, d).wait_send()
                second_copy(mm, d).wait_send()

    def strip_of(mm, slot):
        n = nbr[a * 16 + slot]
        owner = lax.div(n, 4)
        place = lax.div(owner, 4) if mm == 0 else lax.rem(owner, 4)
        return r2[rd][mm][place, slot]

    return finish, strip_of


def zero_corners(pad):
    blank = jnp.zeros((32, 256), F32)
    pad[0] = blank
    pad[17] = blank


def stage_tile(k, tile, strips, pad, shifted):
    pad[1:17, 8:24, :] = tile.astype(F32).reshape(16, 16, 256)
    pad[0, 8:24, :] = strips[0].astype(F32)
    pad[17, 8:24, :] = strips[1].astype(F32)
    pad[1:17, 7, :] = strips[2].astype(F32)
    pad[1:17, 24, :] = strips[3].astype(F32)
    for j in range(3):
        shifted[j, k] = pad[:, 7 + j : 23 + j, :].astype(BF).reshape(288, 256)


def convolve(shifted, filt, bias):
    total = None
    for offset in range(9):
        i, j = divmod(offset, 3)
        part = dot(shifted[j, :, i * 16 : i * 16 + 256, :].reshape(1024, 256), filt[offset])
        total = part if total is None else total + part
    return gelu(total + bias[...])


def greet(pairs_to, pairs_from, ring):
    barrier = pltpu.get_barrier_semaphore()
    a, o, x, z = coordinates()
    if ring:
        for mm in range(2):
            for d in (1, 2, 3):
                target, _ = axis_partner(mm, 0, d)
                pl.semaphore_signal(barrier, inc=1, device_id=target, device_id_type=MESH)

    @pl.loop(0, 16)
    def _(i):
        ta, to = pairs_from(i)

        @pl.when(jnp.logical_or(ta != a, to != o))
        def _():
            pl.semaphore_signal(barrier, inc=1, device_id=(ta, to), device_id_type=MESH)

    self_copy = jnp.where(lax.div(a, 2) == o, 1, 0)
    pl.semaphore_wait(barrier, (6 if ring else 0) + 16 - self_copy)


def air_kernel(air, filt, bias, flux_t, split, nbr, bits,
               first, halo, flux_all,
               square, pad, shifted, g00, g01, g10, g11, st, r00, r01, r10, r11,
               flux_own, flux_in, send, recv, fsend, frecv):
    g1 = ((g00, g01), (g10, g11))
    r2 = ((r00, r01), (r10, r11))
    a, o, x, z = coordinates()

    def flux_to(i):
        return 2 * o + lax.div(i, 8), lax.rem(i, 8)

    def flux_from(i):
        return i, lax.div(a, 2)

    greet(flux_to, flux_from, True)
    zero_corners(pad)
    finish, strip_of = rim_exchange(0, air, nbr, square, g1, st, r2, send, recv)
    finish()
    lane = lax.broadcasted_iota(jnp.int32, (16, 128), 1)
    for mm in range(2):
        @pl.loop(0, 4)
        def _(k):
            strips = [strip_of(mm, k * 4 + s) for s in range(4)]
            stage_tile(k, air[mm, k], strips, pad, shifted)

        first[mm] = (air[mm].astype(F32).reshape(1024, 256)
                     + convolve(shifted, filt, bias)).astype(BF).reshape(4, 256, 256)

        @pl.loop(0, 4)
        def _(k):
            flux = lax.dot_general(flux_t[...], first[mm, k], (((1,), (1,)), ((), ())),
                                   preferred_element_type=F32).astype(BF)
            quads = dot(flux, split[...])
            low = bits[a * 8 + k * 2]
            high = bits[a * 8 + k * 2 + 1]
            chosen = jnp.where(lane < 64, low, high)
            flux_own[mm, pl.ds(pl.multiple_of(k * 16, 16), 16)] = jnp.where(
                chosen == 1, quads[:, 128:], quads[:, :128]).astype(BF)

    def flux_copy(i):
        return pltpu.make_async_remote_copy(
            src_ref=flux_own.at[lax.div(i, 8)], dst_ref=flux_in.at[a],
            send_sem=fsend.at[i], recv_sem=frecv.at[a],
            device_id=flux_to(i), device_id_type=MESH)

    def arrival(i):
        return pltpu.make_async_remote_copy(
            src_ref=flux_own.at[0], dst_ref=flux_in.at[i],
            send_sem=fsend.at[i], recv_sem=frecv.at[i],
            device_id=flux_to(i), device_id_type=MESH)

    @pl.loop(0, 16)
    def _(i):
        ta, to = flux_to(i)
        mine = jnp.logical_and(ta == a, to == o)

        @pl.when(mine)
        def _():
            flux_in[a] = flux_own[lax.div(i, 8)]

        @pl.when(jnp.logical_not(mine))
        def _():
            flux_copy(i).start()

    finish, strip_of = rim_exchange(1, first, nbr, square, g1, st, r2, send, recv)

    @pl.loop(0, 16)
    def _(i):
        ta, to = flux_from(i)

        @pl.when(jnp.logical_or(ta != a, to != o))
        def _():
            arrival(i).wait_recv()

    flux_all[...] = flux_in[...]
    finish()
    for mm in range(2):
        @pl.loop(0, 16)
        def _(slot):
            halo[mm, slot] = strip_of(mm, slot)

    @pl.loop(0, 16)
    def _(i):
        ta, to = flux_to(i)

        @pl.when(jnp.logical_or(ta != a, to != o))
        def _():
            flux_copy(i).wait_send()


def ocean_kernel(marine, sea, sea_all, rims, flux_all, exchange, up, up_rim, pick, mean,
                 wide, wide_bias, gain, entry, entry_bias, leave, skin_t, nbr, quarter,
                 advanced, coarse,
                 strips, sems, fluxes, rim_flux, fine, fine_rim, rim_sea, rim_wet, wet32,
                 pad, depth, forced_all, normed_all):
    o = lax.axis_index("ocn")
    base = o * 16

    def strip_copy(t, s):
        n = nbr[(base + t) * 4 + s]
        start = (1 - s if s < 2 else 5 - s) * 48
        return pltpu.make_async_copy(
            rims.at[n, pl.ds(start, 48)], strips.at[t, s], sems.at[t, s])

    @pl.loop(0, 16)
    def _(t):
        for s in range(4):
            strip_copy(t, s).start()

    wet32[...] = sea_all[...].astype(F32)
    lane = lax.broadcasted_iota(jnp.int32, (16, 128), 1)

    def quadrant(tile):
        q = quarter[tile]
        both = flux_all[lax.div(q, 4)].astype(F32)
        upper = lax.rem(lax.div(q, 2), 2)
        moved = jnp.where(upper == 1, pltpu.roll(both, 64, 1), both)
        return jnp.where(lane < 64, moved, 0.0).astype(BF)

    @pl.loop(0, 16)
    def _(t):
        rows = pl.ds(pl.multiple_of(t * 16, 16), 16)
        fluxes[rows, :] = quadrant(base + t)
        for s in range(4):
            n = nbr[(base + t) * 4 + s]
            rim_flux[rows, s * 128 : (s + 1) * 128] = quadrant(n)
            rim_sea[pl.ds(t, 1), s * 256 : (s + 1) * 256] = wet32[pl.ds(n, 1), :]

    fine[...] = dot(fluxes[...], up[...]).astype(BF)
    fine_rim[...] = dot(rim_flux[...], up_rim[...])
    rim_wet[...] = dot(rim_sea[...].astype(BF), pick[...])
    share = jnp.full((16, 256), 0.0625, BF)
    pad[...] = jnp.zeros(pad.shape, F32)

    @pl.loop(0, 16)
    def _(t):
        rows = pl.ds(pl.multiple_of(t * 16, 16), 16)
        row = jnp.broadcast_to(sea[pl.ds(t, 1), :].astype(F32), (16, 256)).astype(BF)
        wet = dot_t(row, share)
        forced = marine[t].astype(F32) + dot_t(fine[rows, :], exchange[...])
        forced_all[t] = forced
        pad[3:19, 8:24, :] = (forced * wet).astype(BF).astype(F32).reshape(16, 16, 256)
        rim_in = (fine_rim[rows, :] * rim_wet[pl.ds(t, 1), :]).astype(BF)
        extra = dot_t(rim_in, exchange[...])
        for s in range(4):
            strip_copy(t, s).wait()

        def strip(s):
            value = strips[t, s].astype(F32) + extra[s * 64 : s * 64 + 48]
            return value.astype(BF).astype(F32)

        pad[0:3, 8:24, :] = strip(0).reshape(3, 16, 256)
        pad[19:22, 8:24, :] = strip(1).reshape(3, 16, 256)
        west = strip(2)
        east = strip(3)
        for j in range(3):
            pad[3:19, 5 + j, :] = west[16 * j : 16 * j + 16]
            pad[3:19, 24 + j, :] = east[16 * j : 16 * j + 16]
        for g in range(2):
            lanes = slice(g * 128, g * 128 + 128)
            for top in (0, 8):
                total = jnp.broadcast_to(wide_bias[:, lanes].reshape(1, 1, 128), (8, 16, 128))
                for j in range(7):
                    cols = pad[top : top + 14, 5 + j : 21 + j, lanes]
                    for i in range(7):
                        weight = wide[pl.ds(i * 7 + j, 1), lanes].reshape(1, 1, 128)
                        total = total + cols[i : i + 8] * weight
                depth[top * 16 : top * 16 + 128, lanes] = total.reshape(128, 128)
        value = depth[...]
        center = jnp.mean(value, axis=1, keepdims=True)
        value = value - center
        spread = jnp.mean(value * value, axis=1, keepdims=True)
        normed_all[t] = (value * lax.rsqrt(spread + 1e-6) * gain[...]).astype(BF)

    @pl.loop(0, 8)
    def _(p):
        two = pl.ds(p * 2, 2)
        inner = dot(normed_all[two].reshape(512, 256), entry[...]) + entry_bias[...]
        outer = dot(gelu(inner).astype(BF), leave[...])
        pair = jnp.zeros((16, 128), F32)
        for h in range(2):
            t = p * 2 + h
            row = jnp.broadcast_to(sea[pl.ds(t, 1), :].astype(F32), (16, 256)).astype(BF)
            wet = dot_t(row, share)
            result = (wet * (forced_all[t] + outer[h * 256 : h * 256 + 256])).astype(BF)
            advanced[t] = result
            surface = lax.dot_general(skin_t[...], result, (((1,), (1,)), ((), ())),
                                      preferred_element_type=F32).astype(BF)
            pair = pair + dot(surface, mean[h])
        coarse[p] = pair.astype(BF)


def return_kernel(coarse, first, halo, filt, bias, back, join, strip_sel, nbr, inverse, bits,
                  result,
                  held, pad, shifted, second, centre_q, rim_q, centre, rim, send, recv):
    a, o, x, z = coordinates()

    def skin_to(i):
        return i, lax.div(a, 2)

    def skin_from(i):
        return 2 * o + lax.div(i, 8), lax.rem(i, 8)

    greet(skin_to, skin_from, False)

    def skin_copy(i):
        return pltpu.make_async_remote_copy(
            src_ref=coarse, dst_ref=held.at[lax.rem(a, 2), o],
            send_sem=send.at[i], recv_sem=recv.at[lax.rem(a, 2) * 8 + o],
            device_id=skin_to(i), device_id_type=MESH)

    def arrival(i):
        return pltpu.make_async_remote_copy(
            src_ref=coarse, dst_ref=held.at[lax.div(i, 8), lax.rem(i, 8)],
            send_sem=send.at[i], recv_sem=recv.at[i],
            device_id=skin_to(i), device_id_type=MESH)

    @pl.loop(0, 16)
    def _(i):
        ta, to = skin_to(i)
        mine = jnp.logical_and(ta == a, to == o)

        @pl.when(mine)
        def _():
            held[lax.rem(a, 2), o] = coarse[...]

        @pl.when(jnp.logical_not(mine))
        def _():
            skin_copy(i).start()

    zero_corners(pad)

    @pl.loop(0, 16)
    def _(i):
        ta, to = skin_from(i)

        @pl.when(jnp.logical_or(ta != a, to != o))
        def _():
            arrival(i).wait_recv()

    lane = lax.broadcasted_iota(jnp.int32, (16, 128), 1)

    def half(mm, j):
        s = inverse[j]
        b = bits[j]
        both = held[mm, lax.div(s, 16), lax.div(lax.rem(s, 16), 2)].astype(F32)
        moved = jnp.where(lax.rem(s, 2) == b, both, pltpu.roll(both, 64, 1))
        inside = jnp.where(lane < 64, 0, 1) == b
        return jnp.where(inside, moved, 0.0).astype(BF)

    for mm in range(2):
        @pl.loop(0, 4)
        def _(k):
            rows = pl.ds(pl.multiple_of(mm * 64 + k * 16, 16), 16)
            tile = a * 4 + k
            for h in range(2):
                centre_q[rows, h * 128 : h * 128 + 128] = half(mm, tile * 2 + h)
                for s in range(4):
                    n = nbr[tile * 4 + s]
                    at = s * 256 + h * 128
                    rim_q[rows, at : at + 128] = half(mm, n * 2 + h)

    centre[...] = dot(centre_q[...], join[...]).astype(BF)
    rim[...] = dot(rim_q[...], strip_sel[...]).astype(BF)
    for mm in range(2):
        @pl.loop(0, 4)
        def _(k):
            rows = pl.ds(pl.multiple_of(mm * 64 + k * 16, 16), 16)
            tile = (first[mm, k].astype(F32) + dot_t(centre[rows, :], back[...])).astype(BF)
            second[k] = tile
            extra = dot_t(rim[rows, :], back[...])
            strips = [
                (halo[mm, k * 4 + s].astype(F32) + extra[s * 16 : s * 16 + 16]).astype(BF)
                for s in range(4)
            ]
            stage_tile(k, tile, strips, pad, shifted)

        result[mm] = (second[...].astype(F32).reshape(1024, 256)
                      + convolve(shifted, filt, bias)).astype(BF).reshape(4, 256, 256)

    @pl.loop(0, 16)
    def _(i):
        ta, to = skin_to(i)

        @pl.when(jnp.logical_or(ta != a, to != o))
        def _():
            skin_copy(i).wait_send()


def on_device(
    air_member_values,
    marine_member_values,
    air_neighbour_faces,
    marine_neighbour_faces,
    marine_spanned_quarter,
    water_cell_indicator,
    initial_air_filter,
    initial_filter_offset,
    later_air_filter,
    later_filter_offset,
    air_to_exchange_matrix,
    exchange_to_marine_matrix,
    marine_wide_filter,
    wide_filter_offset,
    marine_rescale_factor,
    hidden_entry_matrix,
    hidden_entry_offset,
    hidden_exit_matrix,
    marine_to_skin_matrix,
    skin_to_air_matrix,
):
    split, join, strip_sel, up, up_rim, pick, mean = quarter_tables()
    limit = 56 * 1024 * 1024
    marine = marine_member_values.reshape(16, 256, 256)
    sea = water_cell_indicator
    rims = pl.pallas_call(
        rims_kernel,
        out_shape=jax.ShapeDtypeStruct((16, 192, 256), BF),
        in_specs=[VMEM, VMEM],
        out_specs=VMEM,
        scratch_shapes=[pltpu.VMEM((16, 16, 256), F32)],
        compiler_params=pltpu.CompilerParams(vmem_limit_bytes=limit),
    )(marine, sea)
    rims_all = lax.all_gather(rims, "ocn", axis=0, tiled=True)
    sea_all = lax.all_gather(sea.astype(BF), "ocn", axis=0, tiled=True)

    air_nbr = air_neighbour_faces.reshape(256)
    ocean_nbr = marine_neighbour_faces.reshape(512)
    pair = marine_spanned_quarter // 2
    match = pair[None, :] == jnp.arange(128, dtype=jnp.int32)[:, None]
    inverse = jnp.sum(jnp.where(match, jnp.arange(128, dtype=jnp.int32)[None, :], 0), axis=1)
    bits = jnp.sum(jnp.where(match, (marine_spanned_quarter % 2)[None, :], 0), axis=1)

    first, halo, flux_all = pl.pallas_call(
        air_kernel,
        out_shape=(
            jax.ShapeDtypeStruct((2, 4, 256, 256), BF),
            jax.ShapeDtypeStruct((2, 16, 16, 256), BF),
            jax.ShapeDtypeStruct((16, 64, 128), BF),
        ),
        in_specs=[VMEM] * 5 + [SMEM] * 2,
        out_specs=(VMEM, VMEM, VMEM),
        scratch_shapes=[
            pltpu.VMEM((16, 16, 256), F32),
            pltpu.VMEM((18, 32, 256), F32),
            pltpu.VMEM((3, 4, 288, 256), BF),
        ] + [pltpu.VMEM((4, 16, 16, 256), BF)] * 4 + [
            pltpu.VMEM((2, 2, 3, 16, 16, 256), BF),
        ] + [pltpu.VMEM((4, 16, 16, 256), BF)] * 4 + [
            pltpu.VMEM((2, 64, 128), BF),
            pltpu.VMEM((16, 64, 128), BF),
            pltpu.SemaphoreType.DMA((2, 2, 2, 3)),
            pltpu.SemaphoreType.DMA((2, 2, 2, 3)),
            pltpu.SemaphoreType.DMA((16,)),
            pltpu.SemaphoreType.DMA((16,)),
        ],
        compiler_params=pltpu.CompilerParams(
            collective_id=0, has_side_effects=True, vmem_limit_bytes=limit),
    )(air_member_values, initial_air_filter, initial_filter_offset.reshape(1, 256),
      air_to_exchange_matrix.T, split, air_nbr, bits)

    advanced, coarse = pl.pallas_call(
        ocean_kernel,
        out_shape=(
            jax.ShapeDtypeStruct((16, 256, 256), BF),
            jax.ShapeDtypeStruct((8, 16, 128), BF),
        ),
        in_specs=[VMEM, VMEM, VMEM, HBM] + [VMEM] * 13 + [SMEM] * 2,
        out_specs=(VMEM, VMEM),
        scratch_shapes=[
            pltpu.VMEM((16, 4, 48, 256), BF),
            pltpu.SemaphoreType.DMA((16, 4)),
            pltpu.VMEM((256, 128), BF),
            pltpu.VMEM((256, 512), BF),
            pltpu.VMEM((256, 256), BF),
            pltpu.VMEM((256, 256), F32),
            pltpu.VMEM((16, 1024), F32),
            pltpu.VMEM((16, 256), F32),
            pltpu.VMEM((128, 256), F32),
            pltpu.VMEM((22, 32, 256), F32),
            pltpu.VMEM((256, 256), F32),
            pltpu.VMEM((16, 256, 256), F32),
            pltpu.VMEM((16, 256, 256), BF),
        ],
        compiler_params=pltpu.CompilerParams(vmem_limit_bytes=limit),
    )(marine, sea, sea_all, rims_all, flux_all.reshape(64, 16, 128), exchange_to_marine_matrix,
      up, up_rim, pick, mean, marine_wide_filter.astype(F32), wide_filter_offset.reshape(1, 256),
      marine_rescale_factor.reshape(1, 256), hidden_entry_matrix,
      hidden_entry_offset.reshape(1, 1024), hidden_exit_matrix, marine_to_skin_matrix.T,
      ocean_nbr, marine_spanned_quarter)

    atm_next = pl.pallas_call(
        return_kernel,
        out_shape=jax.ShapeDtypeStruct((2, 4, 256, 256), BF),
        in_specs=[VMEM] * 8 + [SMEM] * 3,
        out_specs=VMEM,
        scratch_shapes=[
            pltpu.VMEM((2, 8, 8, 16, 128), BF),
            pltpu.VMEM((18, 32, 256), F32),
            pltpu.VMEM((3, 4, 288, 256), BF),
            pltpu.VMEM((4, 256, 256), BF),
            pltpu.VMEM((128, 256), BF),
            pltpu.VMEM((128, 1024), BF),
            pltpu.VMEM((128, 256), BF),
            pltpu.VMEM((128, 128), BF),
            pltpu.SemaphoreType.DMA((16,)),
            pltpu.SemaphoreType.DMA((16,)),
        ],
        compiler_params=pltpu.CompilerParams(
            collective_id=1, has_side_effects=True, vmem_limit_bytes=limit),
    )(coarse, first, halo, later_air_filter, later_filter_offset.reshape(1, 256),
      skin_to_air_matrix, join, strip_sel, air_nbr, inverse, bits)
    return atm_next, advanced.reshape(1, 16, 256, 256)


def solution(mesh):
    in_specs = (
        P("ocn", "atm", None, None),
        P("atm", "ocn", None, None),
        P(),
        P(),
        P(),
        P("ocn", None),
    ) + (P(),) * 14
    out_specs = (P("ocn", "atm", None, None), P("atm", "ocn", None, None))
    return jax.shard_map(
        on_device, mesh=mesh, in_specs=in_specs, out_specs=out_specs, check_vma=False
    )
```

time: 537 us -> 195 us (0.36)
  the two profiles are of different devices: /device:TPU:1 before, /device:TPU:100 now
where the time goes in v1:
time: 195 us
  Pallas kernels  155 us (79%)
  blocking collectives  21.2 us (11%)
  between operations  14.1 us (7%)
  local copies, waits for them, and re-layouts  3.8 us (2%)
    pallas_call x1, Pallas kernels, on_device(): pl.pallas_call(ocean_kernel, out_shape=(jax.ShapeDtypeStruct((16, 256, 25...  63.3 us
    pallas_call x1, Pallas kernels, on_device(): pl.pallas_call(air_kernel, out_shape=(jax.ShapeDtypeStruct((2, 4, 256, 25...  53.4 us
    pallas_call x1, Pallas kernels, on_device(): pl.pallas_call(return_kernel, out_shape=jax.ShapeDtypeStruct((2, 4, 256,...  30.3 us
    all_gather x1, blocking collectives, on_device(): sea_all = lax.all_gather(sea.astype(BF), 'ocn', axis=0, tiled=True)  21.2 us
    pallas_call x1, Pallas kernels, on_device(): pl.pallas_call(rims_kernel, out_shape=jax.ShapeDtypeStruct((16, 192, 256)...  7.63 us
  transfers between devices with their start and end apart: 1, of which 0 were waited for; matrix products, arithmetic and copies ran while one was open for 1% of the time, Pallas kernels for 27%

profile of v1, /device:TPU:100, one launch (start us, length us, event | category | flops | bytes accessed | tf_op | source)
XLA Modules:
  0.0 195.2 jit_solution(9651952674528794340)
XLA Ops:
  7.2 0.0 all-gather.2.cloned.1.call-start
  7.2 0.0 copy-start
  7.2 0.0 copy-start.2
  7.2 0.0 copy-start.1
  7.2 0.0 copy-start.3
  7.3 0.0 copy-start.4
  7.3 7.6 %shard_map.266 = bf16[16,192,256]{2,1,0:T(8,128)(2,1)} custom-call(bf16[16,256,256]{2,1,0:T(8,128)(2,1)} %bitcast.10, s32[16,256]{1,0:T(8,128)} %sea.3), custom_call_target="tpu_custom_call" | custom-call | tf_op jit(solution)/shard_map/pallas_call | solution.py:539
  14.9 0.0 all-gather.2.cloned.1.call-update
  14.9 0.0 copy-done
  14.9 0.0 copy-done.2
  15.0 0.1 copy.33
  15.1 0.6 reshape.38.nbr
  15.7 0.0 copy-done.1
  15.7 0.6 convert_element_type.7.wide
  16.3 0.0 copy-done.3
  16.3 0.1 copy.34
  16.4 0.7 reshape.43.nbr
  17.1 0.0 copy-done.4
  17.1 0.7 select_reduce_fusion
  17.8 53.4 %shard_map.267 = (bf16[2,4,256,256]{3,2,1,0:T(8,128)(2,1)}, bf16[2,16,16,256]{3,2,1,0:T(8,128)(2,1)}, bf16[16,64,128]{2,1,0:T(8,128)(2,1)}) custom-call(bf16[2,4,256,256]{3,2,1,0:T(8,128)(2,1)} %air.1, bf16[9,256,256]{2,1,0:T(8,128)(2,1)} %filt.2, f32[1,256]{1,0:T(1,128)} %bitcast.16, bf16[16,256]{1,0:T(8,128)(2,1)} %bitcast.14, ...), custom_call_target="tpu_custom_call" | custom-call | tf_op jit(solution)/shard_map/pallas_call | solution.py:557
  71.2 21.2 %all_gather.6.sea_all = bf16[128,256]{1,0:T(8,128)(2,1)} all-gather(bf16[16,256]{1,0:T(8,128)(2,1)S(1)} %convert_element_type.6), channel_id=1, replica_groups=mesh['atm'=16,'ocn'=8] {'ocn'}, dimensions={0}, use_global_device_ids=true | all-gather | bytes 73728 | tf_op jit(solution)/shard_map/all_gather | solution.py:548
  92.5 0.0 all-gather.2.cloned.1.call-done.rims
  92.5 63.3 %shard_map.268 = (bf16[16,256,256]{2,1,0:T(8,128)(2,1)}, bf16[8,16,128]{2,1,0:T(8,128)(2,1)}) custom-call(bf16[16,256,256]{2,1,0:T(8,128)(2,1)} %bitcast.11, s32[16,256]{1,0:T(8,128)} %sea.3, bf16[128,256]{1,0:T(8,128)(2,1)} %all_gather.6.sea_all, bf16[128,192,256]{2,1,0:T(8,128)(2,1)} %all-gather.2.cloned.1.call-done.rims, bf16[64,16,128]{2,1,0:T(8,128)(2,1)} %bitcast.12, ...), custom_call_target="tpu_custom_call" | custom-call | tf_op jit(solution)/shard_map/pallas_call | solution.py:585
  155.8 30.3 %shard_map.269 = bf16[2,4,256,256]{3,2,1,0:T(8,128)(2,1)} custom-call(bf16[8,16,128]{2,1,0:T(8,128)(2,1)} %get-tuple-element.8.coarse, bf16[2,4,256,256]{3,2,1,0:T(8,128)(2,1)} %get-tuple-element.9.first, bf16[2,16,16,256]{3,2,1,0:T(8,128)(2,1)} %get-tuple-element.10.halo, bf16[9,256,256]{2,1,0:T(8,128)(2,1)} %filt.3, f32[1,256]{1,0:T(1,128)} %bitcast.19, ...), custom_call_target="tpu_custom_call" | custom-call | tf_op jit(solution)/shard_map/pallas_call | solution.py:615
  186.1 2.3 %copy.36 = bf16[2,4,256,256]{3,2,1,0:T(8,128)(2,1)} copy(bf16[2,4,256,256]{3,2,1,0:T(8,128)(2,1)} %shard_map.269) | data formatting | bytes 2097152
  (2 shorter events, 0.0 us)
Async XLA Ops:
  7.2 85.3 %all-gather.2.cloned.1.call-start = ((), (), s32[]{:S(2)}) async-start(), calls=%async_computation | async-start | bytes 14155776 | tf_op jit(solution)/shard_map/all_gather | solution.py:547
  7.2 7.7 %copy-start = (s32[16,256]{1,0:T(8,128)S(1)}, s32[16,256]{1,0:T(8,128)}, u32[]{:S(2)}) copy-start(s32[16,256]{1,0:T(8,128)} %sea.3) | copy-start | bytes 49156
  7.2 7.7 %copy-start.2 = (s32[64,4]{0,1:T(4,128)S(1)}, s32[64,4]{0,1:T(4,128)}, u32[]{:S(2)}) copy-start(s32[64,4]{0,1:T(4,128)} %param.29) | copy-start | bytes 3076
  7.2 8.5 %copy-start.1 = (bf16[49,256]{1,0:T(8,128)(2,1)S(1)}, bf16[49,256]{1,0:T(8,128)(2,1)}, u32[]{:S(2)}) copy-start(bf16[49,256]{1,0:T(8,128)(2,1)} %param.39) | copy-start | bytes 75268
  7.2 9.1 %copy-start.3 = (s32[128,4]{0,1:T(4,128)S(1)}, s32[128,4]{0,1:T(4,128)}, u32[]{:S(2)}) copy-start(s32[128,4]{0,1:T(4,128)} %param.30) | copy-start | bytes 6148
  7.3 9.8 %copy-start.4 = (s32[128]{0:T(128)S(1)}, s32[128]{0:T(128)}, u32[]{:S(2)}) copy-start(s32[128]{0:T(128)} %quarter.1) | copy-start | bytes 1540
Sparse Core Ops, SparseCore 0:
  15.0 74.3 all-gather.1

commit v2 on v0

v2 whole, which is shorter than its diff:
```python
import jax
import jax.numpy as jnp
import numpy as np
from jax import lax
from jax.experimental import pallas as pl
from jax.experimental.pallas import tpu as pltpu
from jax.sharding import PartitionSpec as P

BF = jnp.bfloat16
F32 = jnp.float32
MESH = pl.DeviceIdType.MESH
VMEM = pl.BlockSpec(memory_space=pltpu.VMEM)
SMEM = pl.BlockSpec(memory_space=pltpu.SMEM)
HBM = pl.BlockSpec(memory_space=pl.ANY)
C0 = 0.7978845608028654
C1 = C0 * 0.044715


def gelu(x):
    half = 0.5 * x
    return half + half * jnp.tanh(x * (C0 + C1 * (x * x)))


def dot(a, b):
    return jnp.dot(a, b, preferred_element_type=F32)


def dot_t(a, b):
    return lax.dot_general(a, b, (((0,), (0,)), ((), ())), preferred_element_type=F32)


def cell_tables():
    split = np.zeros((256, 256), np.float32)
    join = np.zeros((256, 256), np.float32)
    for r in range(16):
        for q in range(16):
            a, b = r // 8, q // 8
            cell = (r % 8) * 8 + q % 8
            split[r * 16 + q, b * 128 + a * 64 + cell] = 1
            join[a * 128 + b * 64 + cell, r * 16 + q] = 1
    air_rim = np.zeros((64, 256), np.float32)
    for c in range(16):
        for kind, cell in enumerate((c, 240 + c, c * 16, c * 16 + 15)):
            air_rim[kind * 16 + c, cell] = 1
    ocean_rim = np.zeros((192, 256), np.float32)
    for j in range(3):
        for c in range(16):
            cells = (j * 16 + c, (13 + j) * 16 + c, c * 16 + j, c * 16 + 13 + j)
            for kind, cell in enumerate(cells):
                ocean_rim[kind * 48 + j * 16 + c, cell] = 1
    strip = np.zeros((4, 256, 128), np.float32)
    for c in range(16):
        for side, cell in enumerate((240 + c, c, c * 16 + 15, c * 16)):
            strip[side, :, side * 16 + c] = join[:, cell]
    up = np.zeros((128, 256), np.float32)
    for r in range(16):
        for q in range(16):
            up[(r // 2) * 8 + q // 2, r * 16 + q] = 1
    pick = np.zeros((4, 256, 256), np.float32)
    for j in range(3):
        for c in range(16):
            cells = ((13 + j) * 16 + c, j * 16 + c, c * 16 + 13 + j, c * 16 + j)
            for side, cell in enumerate(cells):
                pick[side, cell, side * 64 + j * 16 + c] = 1
    up_rim = np.einsum("qc,scd->sqd", up, pick)
    shift = np.zeros((512, 7, 384), np.float32)
    for j in range(7):
        for q in range(16):
            col = q + j
            for r in range(22):
                at = r * 16 + q
                if 3 <= r < 19 and 3 <= col < 19:
                    shift[(r - 3) * 16 + col - 3, j, at] = 1
                elif 3 <= col < 19:
                    side, k = (0, r) if r < 3 else (1, r - 19)
                    shift[256 + side * 64 + k * 16 + col - 3, j, at] = 1
                elif 3 <= r < 19:
                    side, k = (2, col) if col < 3 else (3, col - 19)
                    shift[256 + side * 64 + k * 16 + r - 3, j, at] = 1
    mean = np.zeros((2, 256, 128), np.float32)
    for r in range(16):
        for q in range(16):
            for h in range(2):
                mean[h, r * 16 + q, h * 64 + (r // 2) * 8 + q // 2] = 0.25
    tables = (
        split,
        join,
        air_rim,
        ocean_rim,
        strip.reshape(1024, 128),
        up,
        up_rim.reshape(512, 256),
        pick.reshape(1024, 256),
        shift.reshape(512, 2688),
        mean,
    )
    return tuple(jnp.asarray(table, BF) for table in tables)


def coordinates():
    a = lax.axis_index("atm")
    o = lax.axis_index("ocn")
    return a, o, lax.div(a, 4), lax.rem(a, 4)


def axis_partner(mm, phase, d):
    a, o, x, z = coordinates()
    if (mm + phase) % 2 == 0:
        place = lax.rem(z + d, 4)
        return (x * 4 + place, o), place
    place = lax.rem(x + d, 4)
    return (place * 4 + z, o), place


def coupling_partner(k):
    a, o, x, z = coordinates()
    return 2 * o + k, lax.div(a, 2)


def is_me(k):
    a, o, x, z = coordinates()
    return jnp.logical_and(lax.div(a, 2) == o, lax.rem(a, 2) == k)


def remote(src, dst, send, recv, target):
    return pltpu.make_async_remote_copy(
        src_ref=src, dst_ref=dst, send_sem=send, recv_sem=recv,
        device_id=target, device_id_type=MESH)


def greet():
    barrier = pltpu.get_barrier_semaphore()
    a, o, x, z = coordinates()

    def signal(target):
        pl.semaphore_signal(barrier, inc=1, device_id=target, device_id_type=MESH)

    for d in (1, 2, 3):
        for mm in range(2):
            signal(axis_partner(mm, 0, d)[0])
    for d in range(1, 8):
        signal((a, lax.rem(o + d, 8)))
    for k in range(2):
        @pl.when(jnp.logical_not(is_me(k)))
        def _():
            signal(coupling_partner(k))


def await_greetings():
    a, o, x, z = coordinates()
    pl.semaphore_wait(pltpu.get_barrier_semaphore(), 15 - jnp.where(lax.div(a, 2) == o, 1, 0))


def rim_exchange(rd, tiles, nbr, air_rim, g1, st, r2, send, recv):
    a, o, x, z = coordinates()

    def first_copy(mm, d):
        here = axis_partner(mm, 0, 0)[1]
        part = g1[rd][mm].at[here]
        return remote(part, part, send.at[rd, 0, mm, d - 1], recv.at[rd, 0, mm, d - 1],
                      axis_partner(mm, 0, d)[0])

    def second_copy(mm, d):
        here = axis_partner(mm, 1, 0)[1]
        return remote(st.at[rd, mm, d - 1], r2[rd][mm].at[here], send.at[rd, 1, mm, d - 1],
                      recv.at[rd, 1, mm, d - 1], axis_partner(mm, 1, d)[0])

    def begin(mm):
        here = axis_partner(mm, 0, 0)[1]

        @pl.loop(0, 4)
        def _(k):
            rims = dot(air_rim[...], tiles[mm, k]).astype(BF).reshape(4, 16, 256)
            g1[rd][mm][here, pl.ds(k * 4, 4)] = rims

    def send_first(mm):
        for d in (1, 3, 2):
            first_copy(mm, d).start()

    def middle():
        for mm in range(2):
            for d in (1, 2, 3):
                first_copy(mm, d).wait_recv()
            for d in (2, 1, 3, 0):
                (dest, _), place = axis_partner(mm, 1, d)

                @pl.loop(0, 16, unroll=4)
                def _(slot):
                    n = nbr[lax.rem(slot, 4), dest * 4 + lax.div(slot, 4)]
                    owner = lax.div(n, 4)
                    from_place = lax.rem(owner, 4) if mm == 0 else lax.div(owner, 4)
                    side = lax.rem(slot, 4)
                    kind = side + 1 - 2 * lax.rem(side, 2)
                    strip = g1[rd][mm][from_place, lax.rem(n, 4) * 4 + kind]
                    if d == 0:
                        r2[rd][mm][place, slot] = strip
                    else:
                        st[rd, mm, d - 1, slot] = strip

                if d > 0:
                    second_copy(mm, d).start()

    def finish():
        for mm in range(2):
            for d in (1, 2, 3):
                second_copy(mm, d).wait_recv()
        for mm in range(2):
            for d in (1, 2, 3):
                first_copy(mm, d).wait_send()
                second_copy(mm, d).wait_send()

    def strip_of(mm, slot):
        n = nbr[lax.rem(slot, 4), a * 4 + lax.div(slot, 4)]
        owner = lax.div(n, 4)
        place = lax.div(owner, 4) if mm == 0 else lax.rem(owner, 4)
        return r2[rd][mm][place, slot]

    return begin, middle, finish, strip_of, send_first


def stage_tile(k, tile, strips, pad, shifted):
    pad[1:17, 8:24, :] = tile.astype(F32).reshape(16, 16, 256)
    pad[0, 8:24, :] = strips[0].astype(F32)
    pad[17, 8:24, :] = strips[1].astype(F32)
    pad[1:17, 7, :] = strips[2].astype(F32)
    pad[1:17, 24, :] = strips[3].astype(F32)
    for j in range(3):
        shifted[j, k] = pad[:, 7 + j : 23 + j, :].astype(BF).reshape(288, 256)


def convolve(shifted, filt, bias):
    total = None
    for offset in range(9):
        i, j = divmod(offset, 3)
        part = dot(shifted[j, :, i * 16 : i * 16 + 256, :].reshape(1024, 256), filt[offset])
        total = part if total is None else total + part
    return gelu(total + bias[...])


def interior(tile, wide, bias, pad, moved, depth):
    pad[:, 8:24, :] = tile
    for j in range(7):
        moved[j] = pad[:, 5 + j : 21 + j, :]
    for g in range(2):
        lanes = slice(g * 128, g * 128 + 128)
        start = jnp.broadcast_to(bias[:, lanes], (8, 128))
        for c in (0, 8):
            total = [start] * 16
            for j in range(7):
                rows = [moved[j, r, c : c + 8, lanes] for r in range(16)]
                weights = [wide[i * 7 + j, :, lanes] for i in range(7)]
                for p in range(16):
                    for i in range(7):
                        if 0 <= p + i - 3 < 16:
                            total[p] = total[p] + rows[p + i - 3] * weights[i]
            for p in range(16):
                depth[p, c : c + 8, lanes] = total[p]


def rim_sums(side, strip, wide, pad):
    pad[:, 8:24, :] = strip
    total = [None] * 3
    for shift in range(7):
        part = pad[:, 5 + shift : 21 + shift, :].reshape(3, 2, 8, 256)
        for place in range(3):
            for k in range(3):
                along = k - place if side in (0, 2) else 6 + k - place
                if not 0 <= along < 7 or (k < place) == (side in (0, 2)) and k != place:
                    continue
                i, j = (along, shift) if side < 2 else (shift, along)
                term = part[k] * wide[i * 7 + j][None]
                total[place] = term if total[place] is None else total[place] + term
    return [value.reshape(16, 256) for value in total]


def kernel(air, marine, sea, filt_a_far, bias_a, filt_b_far, bias_b, flux_t, exchange, wide_in,
           wide_bias, gain, entry_far, entry_bias, leave_far, skin_t, back,
           split, join, air_rim, ocean_rim, strip_sel, up, up_rim, pick, shift_far, mean,
           air_nbr, ocean_nbr, quarter, places,
           result, advanced,
           filt_a, filt_b, entry, leave, shift, fetch,
           first, pad_a, shifted, g00, g01, g10, g11, st, r00, r01, r10, r11,
           rims, sea_all, wet32, flux_own, flux_in, skin_in, back_out, back_in,
           wide, weights, pad_o, moved, pad_r, depth, forced,
           fluxes, rim_flux, rim_sea, cells, columns, im2col, centre_q, rim_q,
           asend, arecv, bsend, brecv, ssend, srecv, fsend, frecv, ksend, krecv):
    a, o, x, z = coordinates()
    g1 = ((g00, g01), (g10, g11))
    r2 = ((r00, r01), (r10, r11))
    right = (a, lax.rem(o + 2, 8))
    left = (a, lax.rem(o + 6, 8))
    twin = (a, o + 1 - 2 * lax.rem(o, 2))
    before = lax.rem(o + 6, 8)
    after = lax.rem(o + 2, 8)
    across = lax.rem(o + 4, 8)
    lane = lax.broadcasted_iota(jnp.int32, (16, 128), 1)
    share = jnp.full((16, 256), 0.0625, BF)

    def sea_columns(t):
        row = jnp.broadcast_to(sea[pl.ds(t, 1), :].astype(F32), (16, 256)).astype(BF)
        return dot_t(row, share)

    def rim_copy(block, half, target, n):
        part = rims.at[block, pl.ds(half * 8, 8)]
        return remote(part, part, bsend.at[n], brecv.at[n], target)

    def block_copy(block, n):
        return remote(rims.at[block], rims.at[block], bsend.at[n], brecv.at[n], twin)

    own_copies = [rim_copy(o, 0, right, 0), rim_copy(o, 1, left, 1),
                  rim_copy(o, 1, right, 2), rim_copy(o, 0, left, 3)]
    onward_right = rim_copy(before, 0, right, 4)
    onward_left = rim_copy(after, 1, left, 5)
    twin_copies = [block_copy(o, 6), block_copy(before, 7), block_copy(after, 8),
                   block_copy(across, 9)]

    def sea_copy(d):
        return remote(sea_all.at[o], sea_all.at[o], ssend.at[d - 1], srecv.at[d - 1],
                      (a, lax.rem(o + d, 8)))

    def flux_copy(d):
        part = flux_in.at[pl.ds(8 * o, 8)]
        return remote(part, part, fsend.at[d + 1], frecv.at[d + 1], (a, lax.rem(o + d, 8)))

    def skin_copy(d):
        return remote(skin_in.at[o], skin_in.at[o], ksend.at[d + 1], krecv.at[d + 1],
                      (a, lax.rem(o + d, 8)))

    def first_flux(k):
        return remote(flux_own.at[k], flux_in.at[pl.ds(4 * a, 4)], fsend.at[k], frecv.at[lax.rem(a, 2)],
                      coupling_partner(k))

    def last_skin(k):
        return remote(back_out.at[k], back_in.at[lax.rem(a, 2)], ksend.at[k],
                      krecv.at[lax.rem(a, 2)], coupling_partner(k))

    def unless_me(k, act):
        pl.when(jnp.logical_not(is_me(k)))(act)

    greet()
    fetches = [
        pltpu.make_async_copy(far, near, fetch.at[n])
        for n, (far, near) in enumerate((
            (filt_a_far, filt_a), (shift_far, shift), (entry_far, entry), (leave_far, leave),
            (filt_b_far, filt_b)))
    ]
    for copy in fetches:
        copy.start()
    air_first = rim_exchange(0, air, air_nbr, air_rim, g1, st, r2, asend, arecv)
    air_second = rim_exchange(1, first, air_nbr, air_rim, g1, st, r2, asend, arecv)
    air_first[0](0)
    air_first[0](1)
    sea_all[o] = sea[...].astype(F32).astype(BF)

    @pl.loop(0, 16)
    def _(t):
        wet = (marine[t].astype(F32) * sea_columns(t)).astype(BF)
        rims[o, t] = dot(ocean_rim[...], wet).astype(BF).reshape(4, 48, 256)

    await_greetings()
    air_first[4](0)
    air_first[4](1)
    for copy in own_copies:
        copy.start()
    twin_copies[0].start()
    for d in range(1, 8):
        sea_copy(d).start()

    spread_in = exchange[...].astype(F32)
    weights[...] = jnp.zeros(weights.shape, BF)
    for i in range(7):
        for j in range(7):
            row = wide_in[i * 7 + j : i * 7 + j + 1, :].astype(F32)
            wide[i * 7 + j] = jnp.broadcast_to(row, (8, 256))
            at = (i % 2) * 128 + j * 16
            weights[i // 2, at : at + 16, :] = (spread_in * row).astype(BF)
    pad_o[...] = jnp.zeros(pad_o.shape, F32)
    pad_r[...] = jnp.zeros(pad_r.shape, F32)
    pad_a[...] = jnp.zeros(pad_a.shape, F32)

    def interiors(low, high):
        @pl.loop(low, high)
        def _(t):
            tile = (marine[t].astype(F32) * sea_columns(t)).reshape(16, 16, 256)
            interior(tile, wide, wide_bias, pad_o, moved, depth.at[t])

    interiors(0, 5)
    air_first[1]()
    interiors(5, 11)
    air_first[2]()
    fetches[0].wait()

    for mm in range(2):
        @pl.loop(0, 4)
        def _(k):
            strips = [air_first[3](mm, k * 4 + s) for s in range(4)]
            stage_tile(k, air[mm, k], strips, pad_a, shifted)

        first[mm] = (air[mm].astype(F32).reshape(1024, 256)
                     + convolve(shifted, filt_a, bias_a)).astype(BF).reshape(4, 256, 256)

        @pl.loop(0, 4)
        def _(k):
            flux = lax.dot_general(flux_t[...], first[mm, k], (((1,), (1,)), ((), ())),
                                   preferred_element_type=F32).astype(BF)
            quads = dot(flux, split[...])
            low = lax.rem(places[a * 8 + k * 2], 2)
            high = lax.rem(places[a * 8 + k * 2 + 1], 2)
            chosen = jnp.where(lane < 64, low, high)
            flux_own[mm, k] = jnp.where(
                chosen == 1, quads[:, 128:], quads[:, :128]).astype(BF)

        unless_me(mm, lambda: first_flux(mm).start())

        @pl.when(is_me(mm))
        def _():
            flux_in[pl.ds(4 * a, 4)] = flux_own[mm]

        air_second[0](mm)
        air_second[4](mm)

    own_copies[0].wait_recv()
    onward_right.start()
    own_copies[1].wait_recv()
    onward_left.start()

    interiors(11, 14)
    for k in range(2):
        def arrival():
            remote(flux_own.at[0], flux_in.at[pl.ds(8 * o + 4 * k, 4)], fsend.at[k], frecv.at[k],
                   coupling_partner(k)).wait_recv()
        unless_me(k, arrival)
    for d in range(1, 8):
        flux_copy(d).start()
    interiors(14, 16)
    air_second[1]()
    for d in range(1, 8):
        sea_copy(d).wait_recv()
    wet32[...] = sea_all[...].astype(F32).reshape(128, 1, 256)
    for d in range(1, 8):
        flux_copy(d).wait_recv()

    def quadrant(tile):
        q = quarter[tile]
        both = flux_in[lax.div(q, 4)].astype(F32)
        upper = lax.rem(lax.div(q, 2), 2)
        turned = jnp.where(upper == 1, pltpu.roll(both, 64, 1), both)
        return jnp.where(lane < 64, turned, 0.0).astype(BF)

    @pl.loop(0, 16)
    def _(t):
        rows = pl.ds(pl.multiple_of(t * 16, 16), 16)
        fluxes[rows, :] = quadrant(o * 16 + t)
        for s in range(4):
            n = ocean_nbr[s, o * 16 + t]
            rim_flux[rows, s * 128 : (s + 1) * 128] = quadrant(n)
            rim_sea[pl.ds(t, 1), s * 256 : (s + 1) * 256] = wet32[n]

    fine = dot(fluxes[...], up[...])
    sea_here = jnp.broadcast_to(sea[...].astype(F32).reshape(16, 1, 256), (16, 16, 256))
    cells[:, 0:256] = (fine * sea_here.reshape(256, 256)).astype(BF)
    rim_wet = dot(rim_sea[...].astype(BF), pick[...])
    rim_wet = jnp.broadcast_to(rim_wet.reshape(16, 1, 256), (16, 16, 256)).reshape(256, 256)
    cells[:, 256:512] = (dot(rim_flux[...], up_rim[...]) * rim_wet).astype(BF)
    fine = fine.astype(BF)
    for t in range(16):
        forced[t] = (marine[t].astype(F32) + dot_t(fine[t * 16 : t * 16 + 16], exchange[...]))

    own_copies[2].wait_recv()
    twin_copies[1].start()
    own_copies[3].wait_recv()
    twin_copies[2].start()

    fetches[1].wait()
    columns[:, 112:128, :] = jnp.zeros((16, 16, 384), BF)
    for j in range(7):
        shifts = dot(cells[...], shift[:, j * 384 : j * 384 + 384]).astype(BF)
        columns[:, j * 16 : j * 16 + 16, :] = shifts.reshape(16, 16, 384)

    @pl.loop(0, 16)
    def _(t):
        turned = columns[t].astype(F32).T.astype(BF)
        im2col[t, :, 0:128] = turned
        im2col[t, 0:368, 128:256] = turned[16:384]
        im2col[t, 368:384, 128:256] = jnp.zeros((16, 128), BF)

    onward_right.wait_recv()
    onward_left.wait_recv()
    twin_copies[3].start()

    @pl.loop(0, 4)
    def _(p):
        four = pl.ds(p * 4, 4)
        total = depth[four].reshape(1024, 256)
        for i in range(4):
            total = total + dot(im2col[four, i * 32 : i * 32 + 256, :].reshape(1024, 256),
                                weights[i])
        depth[four] = total.reshape(4, 16, 16, 256)

    for copy in twin_copies:
        copy.wait_recv()

    @pl.loop(0, 16)
    def _(t):
        for s in range(4):
            n = ocean_nbr[s, o * 16 + t]
            kind = s + 1 - 2 * (s % 2)
            strip = rims[lax.div(n, 16), lax.rem(n, 16), kind]
            sums = rim_sums(s, strip.astype(F32).reshape(3, 16, 256), wide, pad_r)
            for place in range(3):
                if s < 2:
                    row = place + 13 * s
                    depth[t, row] = depth[t, row] + sums[place]
                else:
                    col = place + 13 * (s - 2)
                    depth[t, :, col, :] = depth[t, :, col, :] + sums[place]

    fetches[2].wait()
    fetches[3].wait()

    @pl.loop(0, 8)
    def _(p):
        two = pl.ds(p * 2, 2)
        value = depth[two].reshape(512, 256)
        value = value - jnp.mean(value, axis=1, keepdims=True)
        spread = jnp.mean(value * value, axis=1, keepdims=True)
        normed = (value * lax.rsqrt(spread + 1e-6) * gain[...]).astype(BF)
        inner = dot(normed, entry[...]) + entry_bias[...]
        outer = dot(gelu(inner).astype(BF), leave[...])
        pair = jnp.zeros((16, 128), F32)
        for h in range(2):
            t = p * 2 + h
            whole = forced[t] + outer[h * 256 : h * 256 + 256]
            done = (sea_columns(t) * whole).astype(BF)
            advanced[t] = done
            surface = lax.dot_general(skin_t[...], done, (((1,), (1,)), ((), ())),
                                      preferred_element_type=F32).astype(BF)
            pair = pair + dot(surface, mean[h])
        skin_in[o, p] = pair.astype(BF)

    for d in range(1, 8):
        skin_copy(d).start()
    air_second[2]()
    for d in range(1, 8):
        skin_copy(d).wait_recv()

    fetches[4].wait()

    def half(j):
        s = lax.div(places[j], 2)
        b = lax.rem(places[j], 2)
        both = skin_in[lax.div(s, 16), lax.div(lax.rem(s, 16), 2)].astype(F32)
        turned = jnp.where(lax.rem(s, 2) == b, both, pltpu.roll(both, 64, 1))
        inside = jnp.where(lane < 64, 0, 1) == b
        return jnp.where(inside, turned, 0.0).astype(BF)

    @pl.loop(0, 8)
    def _(k):
        rows = pl.ds(pl.multiple_of(k * 16, 16), 16)
        tile = o * 8 + k
        for h in range(2):
            centre_q[rows, h * 128 : h * 128 + 128] = half(tile * 2 + h)
            for s in range(4):
                n = air_nbr[s, tile]
                at = s * 256 + h * 128
                rim_q[rows, at : at + 128] = half(n * 2 + h)

    centre = dot(centre_q[...], join[...]).astype(BF)
    rim = dot(rim_q[...], strip_sel[...]).astype(BF)
    for k in range(2):
        back_out[k, :, 0:256] = centre[k * 64 : k * 64 + 64]
        back_out[k, :, 256:384] = rim[k * 64 : k * 64 + 64]
        unless_me(k, lambda: last_skin(k).start())

        @pl.when(is_me(k))
        def _():
            back_in[k] = back_out[k]

    for mm in range(2):
        def arrival():
            remote(back_out.at[0], back_in.at[mm], ksend.at[mm], krecv.at[mm],
                   coupling_partner(mm)).wait_recv()
        unless_me(mm, arrival)

        @pl.loop(0, 4)
        def _(k):
            rows = pl.ds(pl.multiple_of(k * 16, 16), 16)
            add = dot_t(back_in[mm, rows, 0:256], back[...])
            tile = (first[mm, k].astype(F32) + add).astype(BF)
            result[mm, k] = tile
            extra = dot_t(back_in[mm, rows, 256:384], back[...])
            strips = [
                (air_second[3](mm, k * 4 + s).astype(F32) + extra[s * 16 : s * 16 + 16]).astype(BF)
                for s in range(4)
            ]
            stage_tile(k, tile, strips, pad_a, shifted)

        result[mm] = (result[mm].astype(F32).reshape(1024, 256)
                      + convolve(shifted, filt_b, bias_b)).astype(BF).reshape(4, 256, 256)

    for copy in own_copies + [onward_right, onward_left] + twin_copies:
        copy.wait_send()
    for d in range(1, 8):
        sea_copy(d).wait_send()
        flux_copy(d).wait_send()
        skin_copy(d).wait_send()
    for k in range(2):
        unless_me(k, lambda: first_flux(k).wait_send())
        unless_me(k, lambda: last_skin(k).wait_send())


def on_device(
    air_member_values,
    marine_member_values,
    air_neighbour_faces,
    marine_neighbour_faces,
    marine_spanned_quarter,
    water_cell_indicator,
    initial_air_filter,
    initial_filter_offset,
    later_air_filter,
    later_filter_offset,
    air_to_exchange_matrix,
    exchange_to_marine_matrix,
    marine_wide_filter,
    wide_filter_offset,
    marine_rescale_factor,
    hidden_entry_matrix,
    hidden_entry_offset,
    hidden_exit_matrix,
    marine_to_skin_matrix,
    skin_to_air_matrix,
):
    index = lax.broadcasted_iota(jnp.int32, (128, 128), 0)
    tile = lax.broadcasted_iota(jnp.int32, (128, 128), 1)
    covered = jnp.broadcast_to(marine_spanned_quarter[None, :], (128, 128))
    code = jnp.where((covered >> 1) == index, 2 * tile + (covered & 1), 0)
    places = jnp.sum(code, axis=1)
    strips = pltpu.VMEM((4, 16, 16, 256), BF)
    dma = pltpu.SemaphoreType.DMA
    atm_next, advanced = pl.pallas_call(
        kernel,
        out_shape=(
            jax.ShapeDtypeStruct((2, 4, 256, 256), BF),
            jax.ShapeDtypeStruct((16, 256, 256), BF),
        ),
        in_specs=[VMEM] * 3 + [HBM, VMEM, HBM] + [VMEM] * 6 + [HBM, VMEM, HBM] + [VMEM] * 10
        + [HBM, VMEM] + [SMEM] * 4,
        out_specs=(VMEM, VMEM),
        scratch_shapes=[
            pltpu.VMEM((9, 256, 256), BF),
            pltpu.VMEM((9, 256, 256), BF),
            pltpu.VMEM((256, 1024), BF),
            pltpu.VMEM((1024, 256), BF),
            pltpu.VMEM((512, 2688), BF),
            dma((5,)),
            pltpu.VMEM((2, 4, 256, 256), BF),
            pltpu.VMEM((18, 32, 256), F32),
            pltpu.VMEM((3, 4, 288, 256), BF),
            strips, strips, strips, strips,
            pltpu.VMEM((2, 2, 3, 16, 16, 256), BF),
            strips, strips, strips, strips,
            pltpu.VMEM((8, 16, 4, 48, 256), BF),
            pltpu.VMEM((8, 16, 256), BF),
            pltpu.VMEM((128, 1, 256), F32),
            pltpu.VMEM((2, 4, 16, 128), BF),
            pltpu.VMEM((64, 16, 128), BF),
            pltpu.VMEM((8, 8, 16, 128), BF),
            pltpu.VMEM((2, 64, 384), BF),
            pltpu.VMEM((2, 64, 384), BF),
            pltpu.VMEM((49, 8, 256), F32),
            pltpu.VMEM((4, 256, 256), BF),
            pltpu.VMEM((16, 32, 256), F32),
            pltpu.VMEM((7, 16, 16, 256), F32),
            pltpu.VMEM((3, 32, 256), F32),
            pltpu.VMEM((16, 16, 16, 256), F32),
            pltpu.VMEM((16, 256, 256), F32),
            pltpu.VMEM((256, 128), BF),
            pltpu.VMEM((256, 512), BF),
            pltpu.VMEM((16, 1024), F32),
            pltpu.VMEM((256, 512), BF),
            pltpu.VMEM((16, 128, 384), BF),
            pltpu.VMEM((16, 384, 256), BF),
            pltpu.VMEM((128, 256), BF),
            pltpu.VMEM((128, 1024), BF),
            dma((2, 2, 2, 3)), dma((2, 2, 2, 3)),
            dma((10,)), dma((10,)),
            dma((7,)), dma((7,)),
            dma((9,)), dma((9,)),
            dma((9,)), dma((9,)),
        ],
        compiler_params=pltpu.CompilerParams(
            collective_id=0, has_side_effects=True, vmem_limit_bytes=60 * 1024 * 1024),
    )(
        air_member_values, marine_member_values.reshape(16, 256, 256), water_cell_indicator,
        initial_air_filter, initial_filter_offset.reshape(1, 256),
        later_air_filter, later_filter_offset.reshape(1, 256),
        air_to_exchange_matrix.T, exchange_to_marine_matrix, marine_wide_filter,
        wide_filter_offset.reshape(1, 256), marine_rescale_factor.reshape(1, 256),
        hidden_entry_matrix, hidden_entry_offset.reshape(1, 1024), hidden_exit_matrix,
        marine_to_skin_matrix.T, skin_to_air_matrix, *cell_tables(),
        air_neighbour_faces.T, marine_neighbour_faces.T, marine_spanned_quarter, places,
    )
    return atm_next, advanced.reshape(1, 16, 256, 256)


def solution(mesh):
    in_specs = (
        P("ocn", "atm", None, None),
        P("atm", "ocn", None, None),
        P(),
        P(),
        P(),
        P("ocn", None),
    ) + (P(),) * 14
    out_specs = (P("ocn", "atm", None, None), P("atm", "ocn", None, None))
    return jax.shard_map(
        on_device, mesh=mesh, in_specs=in_specs, out_specs=out_specs, check_vma=False
    )
```

time: 537 us -> 128 us (0.24)
  the two profiles are of different devices: /device:TPU:1 before, /device:TPU:25 now
where the time goes in v2:
time: 128 us
  Pallas kernels  122 us (95%)
  local copies, waits for them, and re-layouts  3.73 us (3%)
  other arithmetic  1.29 us (1%)
    pallas_call x1, Pallas kernels, on_device(): pl.pallas_call(kernel, out_shape=(jax.ShapeDtypeStruct((2, 4, 256, 256),...  122 us
    unnamed x4, local copies, waits for them, and re-layouts  3.73 us

profile of v2, /device:TPU:25, one launch (start us, length us, event | category | flops | bytes accessed | tf_op | source)
XLA Modules:
  0.0 128.1 jit_solution(17976266006199290158)
XLA Ops:
  0.6 0.7 broadcast_shift-right-arithmetic_fusion
  1.3 0.6 select_reduce_fusion.places
  1.9 122.5 %shard_map.293 = (bf16[2,4,256,256]{3,2,1,0:T(8,128)(2,1)}, bf16[16,256,256]{2,1,0:T(8,128)(2,1)}) custom-call(bf16[2,4,256,256]{3,2,1,0:T(8,128)(2,1)} %air.1, bf16[16,256,256]{2,1,0:T(8,128)(2,1)} %bitcast.11, s32[16,256]{1,0:T(8,128)} %sea.1, bf16[9,256,256]{2,1,0:T(8,128)(2,1)} %filt_a_far.1, f32[1,256]{1,0:T(1,128)} %bitcast.18, ...), custom_call_target="tpu_custom_call" | custom-call | tf_op jit(solution)/shard_map/pallas_call | solution.py:641
  124.4 0.0 copy-start
  124.4 2.4 %copy.34 = bf16[2,4,256,256]{3,2,1,0:T(8,128)(2,1)} copy(bf16[2,4,256,256]{3,2,1,0:T(8,128)(2,1)} %get-tuple-element.10) | data formatting | bytes 2097152
  126.8 0.0 copy-done
  126.8 1.3 %copy.35 = bf16[1,16,256,256]{3,2,1,0:T(8,128)(2,1)} copy(bf16[1,16,256,256]{3,2,1,0:T(8,128)(2,1)S(1)} %bitcast.12) | data formatting | bytes 4194304
Async XLA Ops:
  124.4 2.4 %copy-start = (bf16[16,256,256]{2,1,0:T(8,128)(2,1)S(1)}, bf16[16,256,256]{2,1,0:T(8,128)(2,1)}, u32[]{:S(2)}) copy-start(bf16[16,256,256]{2,1,0:T(8,128)(2,1)} %get-tuple-element.5) | copy-start | bytes 6291460

commit v3 on v2

--- a/solution.py
+++ b/solution.py
@@ -42,12 +42,21 @@
     for c in range(16):
         for kind, cell in enumerate((c, 240 + c, c * 16, c * 16 + 15)):
             air_rim[kind * 16 + c, cell] = 1
-    ocean_rim = np.zeros((192, 256), np.float32)
+    ocean_rim = np.zeros((160, 256), np.float32)
+    side_sel = np.zeros((2, 48, 160), np.float32)
     for j in range(3):
         for c in range(16):
-            cells = (j * 16 + c, (13 + j) * 16 + c, c * 16 + j, c * 16 + 13 + j)
-            for kind, cell in enumerate(cells):
-                ocean_rim[kind * 48 + j * 16 + c, cell] = 1
+            ocean_rim[j * 16 + c, j * 16 + c] = 1
+            ocean_rim[48 + j * 16 + c, (13 + j) * 16 + c] = 1
+            for side, (col, start) in enumerate(((13 + j, 128), (j, 96))):
+                at = start + (c - 3) * 3 + j
+                if c < 3:
+                    at = c * 16 + col
+                elif c >= 13:
+                    at = 48 + (c - 13) * 16 + col
+                else:
+                    ocean_rim[at, c * 16 + col] = 1
+                side_sel[side, j * 16 + c, at] = 1
     strip = np.zeros((4, 256, 128), np.float32)
     for c in range(16):
         for side, cell in enumerate((240 + c, c, c * 16 + 15, c * 16)):
@@ -87,6 +96,7 @@
         join,
         air_rim,
         ocean_rim,
+        side_sel,
         strip.reshape(1024, 128),
         up,
         up_rim.reshape(512, 256),
@@ -168,7 +178,7 @@
     def begin(mm):
         here = axis_partner(mm, 0, 0)[1]
 
-        @pl.loop(0, 4)
+        @pl.loop(0, 4, unroll=4)
         def _(k):
             rims = dot(air_rim[...], tiles[mm, k]).astype(BF).reshape(4, 16, 256)
             g1[rd][mm][here, pl.ds(k * 4, 4)] = rims
@@ -275,13 +285,13 @@
 
 def kernel(air, marine, sea, filt_a_far, bias_a, filt_b_far, bias_b, flux_t, exchange, wide_in,
            wide_bias, gain, entry_far, entry_bias, leave_far, skin_t, back,
-           split, join, air_rim, ocean_rim, strip_sel, up, up_rim, pick, shift_far, mean,
+           split, join, air_rim, ocean_rim, side_sel, strip_sel, up, up_rim, pick, shift_far, mean,
            air_nbr, ocean_nbr, quarter, places,
            result, advanced,
            filt_a, filt_b, entry, leave, shift, fetch,
            first, pad_a, shifted, g00, g01, g10, g11, st, r00, r01, r10, r11,
            rims, sea_all, wet32, flux_own, flux_in, skin_in, back_out, back_in,
-           wide, weights, pad_o, moved, pad_r, depth, forced,
+           wide, weights, pad_o, moved, pad_r, depth, normed_even, normed_odd, fine_flux,
            fluxes, rim_flux, rim_sea, cells, columns, im2col, centre_q, rim_q,
            asend, arecv, bsend, brecv, ssend, srecv, fsend, frecv, ksend, krecv):
     a, o, x, z = coordinates()
@@ -312,7 +322,7 @@
     onward_right = rim_copy(before, 0, right, 4)
     onward_left = rim_copy(after, 1, left, 5)
     twin_copies = [block_copy(o, 6), block_copy(before, 7), block_copy(after, 8),
-                   block_copy(across, 9)]
+                   rim_copy(across, 0, twin, 9), rim_copy(across, 1, twin, 10)]
 
     def sea_copy(d):
         return remote(sea_all.at[o], sea_all.at[o], ssend.at[d - 1], srecv.at[d - 1],
@@ -352,10 +362,10 @@
     air_first[0](1)
     sea_all[o] = sea[...].astype(F32).astype(BF)
 
-    @pl.loop(0, 16)
+    @pl.loop(0, 16, unroll=4)
     def _(t):
-        wet = (marine[t].astype(F32) * sea_columns(t)).astype(BF)
-        rims[o, t] = dot(ocean_rim[...], wet).astype(BF).reshape(4, 48, 256)
+        wet = (ocean_rim[...].astype(F32) * sea[pl.ds(t, 1), :].astype(F32)).astype(BF)
+        rims[o, t] = dot(wet, marine[t]).astype(BF)
 
     await_greetings()
     air_first[4](0)
@@ -439,6 +449,10 @@
     wet32[...] = sea_all[...].astype(F32).reshape(128, 1, 256)
     for d in range(1, 8):
         flux_copy(d).wait_recv()
+    own_copies[2].wait_recv()
+    twin_copies[1].start()
+    own_copies[3].wait_recv()
+    twin_copies[2].start()
 
     def quadrant(tile):
         q = quarter[tile]
@@ -462,14 +476,7 @@
     rim_wet = dot(rim_sea[...].astype(BF), pick[...])
     rim_wet = jnp.broadcast_to(rim_wet.reshape(16, 1, 256), (16, 16, 256)).reshape(256, 256)
     cells[:, 256:512] = (dot(rim_flux[...], up_rim[...]) * rim_wet).astype(BF)
-    fine = fine.astype(BF)
-    for t in range(16):
-        forced[t] = (marine[t].astype(F32) + dot_t(fine[t * 16 : t * 16 + 16], exchange[...]))
-
-    own_copies[2].wait_recv()
-    twin_copies[1].start()
-    own_copies[3].wait_recv()
-    twin_copies[2].start()
+    fine_flux[...] = fine.astype(BF)
 
     fetches[1].wait()
     columns[:, 112:128, :] = jnp.zeros((16, 16, 384), BF)
@@ -483,10 +490,6 @@
         im2col[t, :, 0:128] = turned
         im2col[t, 0:368, 128:256] = turned[16:384]
         im2col[t, 368:384, 128:256] = jnp.zeros((16, 128), BF)
-
-    onward_right.wait_recv()
-    onward_left.wait_recv()
-    twin_copies[3].start()
 
     @pl.loop(0, 4)
     def _(p):
@@ -497,46 +500,82 @@
                                 weights[i])
         depth[four] = total.reshape(4, 16, 16, 256)
 
+    onward_right.wait_recv()
+    twin_copies[3].start()
+    onward_left.wait_recv()
+    twin_copies[4].start()
     for copy in twin_copies:
         copy.wait_recv()
 
-    @pl.loop(0, 16)
-    def _(t):
-        for s in range(4):
-            n = ocean_nbr[s, o * 16 + t]
-            kind = s + 1 - 2 * (s % 2)
-            strip = rims[lax.div(n, 16), lax.rem(n, 16), kind]
-            sums = rim_sums(s, strip.astype(F32).reshape(3, 16, 256), wide, pad_r)
-            for place in range(3):
-                if s < 2:
-                    row = place + 13 * s
-                    depth[t, row] = depth[t, row] + sums[place]
-                else:
-                    col = place + 13 * (s - 2)
-                    depth[t, :, col, :] = depth[t, :, col, :] + sums[place]
-
     fetches[2].wait()
     fetches[3].wait()
-
-    @pl.loop(0, 8)
-    def _(p):
-        two = pl.ds(p * 2, 2)
-        value = depth[two].reshape(512, 256)
+    leave[...] = (leave[...].astype(F32) * 0.5).astype(BF)
+
+    def add_rim(t, h, s):
+        n = ocean_nbr[s, o * 16 + t]
+        beside = rims[lax.div(n, 16), lax.rem(n, 16)]
+        if s < 2:
+            strip = beside[48 - 48 * s : 96 - 48 * s].astype(F32)
+        else:
+            strip = dot(side_sel[s - 2], beside)
+        sums = rim_sums(s, strip.reshape(3, 16, 256), wide, pad_r.at[h * 4 + s])
+        for place in range(3):
+            if s < 2:
+                row = place + 13 * s
+                depth[t, row] = depth[t, row] + sums[place]
+            else:
+                col = place + 13 * (s - 2)
+                depth[t, :, col, :] = depth[t, :, col, :] + sums[place]
+
+    def norm(t, h, normed):
+        value = depth[t].reshape(256, 256)
         value = value - jnp.mean(value, axis=1, keepdims=True)
         spread = jnp.mean(value * value, axis=1, keepdims=True)
-        normed = (value * lax.rsqrt(spread + 1e-6) * gain[...]).astype(BF)
-        inner = dot(normed, entry[...]) + entry_bias[...]
-        outer = dot(gelu(inner).astype(BF), leave[...])
+        value = value * lax.rsqrt(spread + 1e-6) * gain[...]
+        normed[h * 256 : h * 256 + 256] = value.astype(BF)
+
+    def emit(p, outer):
         pair = jnp.zeros((16, 128), F32)
         for h in range(2):
             t = p * 2 + h
-            whole = forced[t] + outer[h * 256 : h * 256 + 256]
+            rows = pl.ds(pl.multiple_of(t * 16, 16), 16)
+            forced = marine[t].astype(F32) + dot_t(fine_flux[rows, :], exchange[...])
+            whole = forced + outer[h * 256 : h * 256 + 256]
             done = (sea_columns(t) * whole).astype(BF)
             advanced[t] = done
             surface = lax.dot_general(skin_t[...], done, (((1,), (1,)), ((), ())),
                                       preferred_element_type=F32).astype(BF)
             pair = pair + dot(surface, mean[h])
         skin_in[o, p] = pair.astype(BF)
+
+    def work(p, now, later):
+        outer = None
+        for part in range(4):
+            if now is not None:
+                lanes = slice(part * 256, part * 256 + 256)
+                inner = dot(now[...], entry[:, lanes]) + entry_bias[:, lanes]
+                inner = (inner + inner * jnp.tanh(inner * (C0 + C1 * (inner * inner)))).astype(BF)
+                term = dot(inner, leave[lanes, :])
+                outer = term if outer is None else outer + term
+            if later is not None:
+                for h, s in ((part // 2, part % 2 * 2), (part // 2, part % 2 * 2 + 1)):
+                    add_rim(p * 2 + 2 + h, h, s)
+        if later is not None:
+            for h in range(2):
+                norm(p * 2 + 2 + h, h, later)
+        if now is not None:
+            emit(p, outer)
+
+    even, odd = normed_even, normed_odd
+    work(jnp.int32(-1), None, even)
+
+    @pl.loop(0, 3)
+    def _(q):
+        work(2 * q, even, odd)
+        work(2 * q + 1, odd, even)
+
+    work(jnp.int32(6), even, odd)
+    work(jnp.int32(7), odd, None)
 
     for d in range(1, 8):
         skin_copy(d).start()
@@ -644,7 +683,7 @@
             jax.ShapeDtypeStruct((2, 4, 256, 256), BF),
             jax.ShapeDtypeStruct((16, 256, 256), BF),
         ),
-        in_specs=[VMEM] * 3 + [HBM, VMEM, HBM] + [VMEM] * 6 + [HBM, VMEM, HBM] + [VMEM] * 10
+        in_specs=[VMEM] * 3 + [HBM, VMEM, HBM] + [VMEM] * 6 + [HBM, VMEM, HBM] + [VMEM] * 11
         + [HBM, VMEM] + [SMEM] * 4,
         out_specs=(VMEM, VMEM),
         scratch_shapes=[
@@ -660,7 +699,7 @@
             strips, strips, strips, strips,
             pltpu.VMEM((2, 2, 3, 16, 16, 256), BF),
             strips, strips, strips, strips,
-            pltpu.VMEM((8, 16, 4, 48, 256), BF),
+            pltpu.VMEM((8, 16, 160, 256), BF),
             pltpu.VMEM((8, 16, 256), BF),
             pltpu.VMEM((128, 1, 256), F32),
             pltpu.VMEM((2, 4, 16, 128), BF),
@@ -672,9 +711,11 @@
             pltpu.VMEM((4, 256, 256), BF),
             pltpu.VMEM((16, 32, 256), F32),
             pltpu.VMEM((7, 16, 16, 256), F32),
-            pltpu.VMEM((3, 32, 256), F32),
+            pltpu.VMEM((8, 3, 32, 256), F32),
             pltpu.VMEM((16, 16, 16, 256), F32),
-            pltpu.VMEM((16, 256, 256), F32),
+            pltpu.VMEM((512, 256), BF),
+            pltpu.VMEM((512, 256), BF),
+            pltpu.VMEM((256, 256), BF),
             pltpu.VMEM((256, 128), BF),
             pltpu.VMEM((256, 512), BF),
             pltpu.VMEM((16, 1024), F32),
@@ -684,7 +725,7 @@
             pltpu.VMEM((128, 256), BF),
             pltpu.VMEM((128, 1024), BF),
             dma((2, 2, 2, 3)), dma((2, 2, 2, 3)),
-            dma((10,)), dma((10,)),
+            dma((11,)), dma((11,)),
             dma((7,)), dma((7,)),
             dma((9,)), dma((9,)),
             dma((9,)), dma((9,)),

time: 128 us -> 114 us (0.89)
  Pallas kernels: 122 us -> 108 us
    pallas_call x1, Pallas kernels: 122 us -> 108 us  [on_device(): pl.pallas_call(kernel, out_shape=(jax.ShapeDtypeStruct((2, 4, 256, 256),...]
where the time goes in v3:
time: 114 us
  Pallas kernels  108 us (95%)
  local copies, waits for them, and re-layouts  3.73 us (3%)
  other arithmetic  1.29 us (1%)
    pallas_call x1, Pallas kernels, on_device(): pl.pallas_call(kernel, out_shape=(jax.ShapeDtypeStruct((2, 4, 256, 256),...  108 us
    unnamed x4, local copies, waits for them, and re-layouts  3.73 us

profile of v3, /device:TPU:25, one launch (start us, length us, event | category | flops | bytes accessed | tf_op | source)
XLA Modules:
  0.0 114.0 jit_solution(9464103700127428720)
XLA Ops:
  0.6 0.7 broadcast_shift-right-arithmetic_fusion
  1.3 0.6 select_reduce_fusion.places
  1.9 108.3 %shard_map.302 = (bf16[2,4,256,256]{3,2,1,0:T(8,128)(2,1)}, bf16[16,256,256]{2,1,0:T(8,128)(2,1)}) custom-call(bf16[2,4,256,256]{3,2,1,0:T(8,128)(2,1)} %air.1, bf16[16,256,256]{2,1,0:T(8,128)(2,1)} %bitcast.11, s32[16,256]{1,0:T(8,128)} %sea.1, bf16[9,256,256]{2,1,0:T(8,128)(2,1)} %filt_a_far.1, f32[1,256]{1,0:T(1,128)} %bitcast.18, ...), custom_call_target="tpu_custom_call" | custom-call | tf_op jit(solution)/shard_map/pallas_call | solution.py:680
  110.3 0.0 copy-start
  110.3 2.4 %copy.35 = bf16[2,4,256,256]{3,2,1,0:T(8,128)(2,1)} copy(bf16[2,4,256,256]{3,2,1,0:T(8,128)(2,1)} %get-tuple-element.10) | data formatting | bytes 2097152
  112.7 0.0 copy-done
  112.7 1.3 %copy.36 = bf16[1,16,256,256]{3,2,1,0:T(8,128)(2,1)} copy(bf16[1,16,256,256]{3,2,1,0:T(8,128)(2,1)S(1)} %bitcast.12) | data formatting | bytes 4194304
Async XLA Ops:
  110.3 2.4 %copy-start = (bf16[16,256,256]{2,1,0:T(8,128)(2,1)S(1)}, bf16[16,256,256]{2,1,0:T(8,128)(2,1)}, u32[]{:S(2)}) copy-start(bf16[16,256,256]{2,1,0:T(8,128)(2,1)} %get-tuple-element.5) | copy-start | bytes 6291460

commit v4 on v3

--- a/solution.py
+++ b/solution.py
@@ -86,6 +86,18 @@
                 elif 3 <= r < 19:
                     side, k = (2, col) if col < 3 else (3, col - 19)
                     shift[256 + side * 64 + k * 16 + r - 3, j, at] = 1
+    shift_air = np.zeros((384, 3, 384), np.float32)
+    for j in range(3):
+        for q in range(16):
+            col = q + j
+            for r in range(18):
+                at = r * 16 + q
+                if 1 <= r < 17 and 1 <= col < 17:
+                    shift_air[(r - 1) * 16 + col - 1, j, at] = 1
+                elif 1 <= col < 17:
+                    shift_air[256 + (0 if r < 1 else 16) + col - 1, j, at] = 1
+                elif 1 <= r < 17:
+                    shift_air[256 + (32 if col < 1 else 48) + r - 1, j, at] = 1
     mean = np.zeros((2, 256, 128), np.float32)
     for r in range(16):
         for q in range(16):
@@ -102,6 +114,7 @@
         up_rim.reshape(512, 256),
         pick.reshape(1024, 256),
         shift.reshape(512, 2688),
+        shift_air.reshape(384, 1152),
         mean,
     )
     return tuple(jnp.asarray(table, BF) for table in tables)
@@ -238,13 +251,13 @@
         shifted[j, k] = pad[:, 7 + j : 23 + j, :].astype(BF).reshape(288, 256)
 
 
-def convolve(shifted, filt, bias):
+def convolve(shifted, filt):
     total = None
     for offset in range(9):
         i, j = divmod(offset, 3)
         part = dot(shifted[j, :, i * 16 : i * 16 + 256, :].reshape(1024, 256), filt[offset])
         total = part if total is None else total + part
-    return gelu(total + bias[...])
+    return total
 
 
 def interior(tile, wide, bias, pad, moved, depth):
@@ -285,7 +298,7 @@
 
 def kernel(air, marine, sea, filt_a_far, bias_a, filt_b_far, bias_b, flux_t, exchange, wide_in,
            wide_bias, gain, entry_far, entry_bias, leave_far, skin_t, back,
-           split, join, air_rim, ocean_rim, side_sel, strip_sel, up, up_rim, pick, shift_far, mean,
+           split, join, air_rim, ocean_rim, side_sel, strip_sel, up, up_rim, pick, shift_far, shift_air, mean,
            air_nbr, ocean_nbr, quarter, places,
            result, advanced,
            filt_a, filt_b, entry, leave, shift, fetch,
@@ -293,6 +306,7 @@
            rims, sea_all, wet32, flux_own, flux_in, skin_in, back_out, back_in,
            wide, weights, pad_o, moved, pad_r, depth, normed_even, normed_odd, fine_flux,
            fluxes, rim_flux, rim_sea, cells, columns, im2col, centre_q, rim_q,
+           sums, field_weights, field_columns, field_cells,
            asend, arecv, bsend, brecv, ssend, srecv, fsend, frecv, ksend, krecv):
     a, o, x, z = coordinates()
     g1 = ((g00, g01), (g10, g11))
@@ -332,9 +346,10 @@
         part = flux_in.at[pl.ds(8 * o, 8)]
         return remote(part, part, fsend.at[d + 1], frecv.at[d + 1], (a, lax.rem(o + d, 8)))
 
-    def skin_copy(d):
-        return remote(skin_in.at[o], skin_in.at[o], ksend.at[d + 1], krecv.at[d + 1],
-                      (a, lax.rem(o + d, 8)))
+    def skin_copy(d, half):
+        part = skin_in.at[o, pl.ds(half * 4, 4)]
+        n = d + 1 + 7 * half
+        return remote(part, part, ksend.at[n], krecv.at[n], (a, lax.rem(o + d, 8)))
 
     def first_flux(k):
         return remote(flux_own.at[k], flux_in.at[pl.ds(4 * a, 4)], fsend.at[k], frecv.at[lax.rem(a, 2)],
@@ -407,7 +422,7 @@
             stage_tile(k, air[mm, k], strips, pad_a, shifted)
 
         first[mm] = (air[mm].astype(F32).reshape(1024, 256)
-                     + convolve(shifted, filt_a, bias_a)).astype(BF).reshape(4, 256, 256)
+                     + gelu(convolve(shifted, filt_a) + bias_a[...])).astype(BF).reshape(4, 256, 256)
 
         @pl.loop(0, 4)
         def _(k):
@@ -429,11 +444,6 @@
         air_second[0](mm)
         air_second[4](mm)
 
-    own_copies[0].wait_recv()
-    onward_right.start()
-    own_copies[1].wait_recv()
-    onward_left.start()
-
     interiors(11, 14)
     for k in range(2):
         def arrival():
@@ -442,6 +452,10 @@
         unless_me(k, arrival)
     for d in range(1, 8):
         flux_copy(d).start()
+    own_copies[0].wait_recv()
+    onward_right.start()
+    own_copies[1].wait_recv()
+    onward_left.start()
     interiors(14, 16)
     air_second[1]()
     for d in range(1, 8):
@@ -500,10 +514,29 @@
                                 weights[i])
         depth[four] = total.reshape(4, 16, 16, 256)
 
+    def early_sums(mm):
+        @pl.loop(0, 4)
+        def _(k):
+            strips = [air_second[3](mm, k * 4 + s) for s in range(4)]
+            stage_tile(k, first[mm, k], strips, pad_a, shifted)
+
+        sums[mm] = convolve(shifted, filt_b)
+
+    air_second[2]()
+    fetches[4].wait()
+    early_sums(0)
+
     onward_right.wait_recv()
     twin_copies[3].start()
     onward_left.wait_recv()
     twin_copies[4].start()
+    field_weights[...] = jnp.zeros(field_weights.shape, BF)
+    for h in range(2):
+        for i in range(3):
+            for j in range(3):
+                at = h * 64 + j * 16
+                field_weights[h, i, at : at + 16] = dot(back[...], filt_b[3 * i + j]).astype(BF)
+    field_columns[...] = jnp.zeros(field_columns.shape, BF)
     for copy in twin_copies:
         copy.wait_recv()
 
@@ -574,16 +607,18 @@
         work(2 * q, even, odd)
         work(2 * q + 1, odd, even)
 
+    for d in range(1, 8):
+        skin_copy(d, 0).start()
     work(jnp.int32(6), even, odd)
     work(jnp.int32(7), odd, None)
 
     for d in range(1, 8):
-        skin_copy(d).start()
-    air_second[2]()
+        skin_copy(d, 1).start()
+    early_sums(1)
+
     for d in range(1, 8):
-        skin_copy(d).wait_recv()
-
-    fetches[4].wait()
+        skin_copy(d, 0).wait_recv()
+        skin_copy(d, 1).wait_recv()
 
     def half(j):
         s = lax.div(places[j], 2)
@@ -621,28 +656,37 @@
                    coupling_partner(mm)).wait_recv()
         unless_me(mm, arrival)
 
-        @pl.loop(0, 4)
-        def _(k):
-            rows = pl.ds(pl.multiple_of(k * 16, 16), 16)
+    for j in range(3):
+        moved_fields = dot(back_in[...].reshape(128, 384), shift_air[:, j * 384 : j * 384 + 384])
+        moved_fields = moved_fields.astype(BF).reshape(4, 2, 16, 384)
+        for h in range(2):
+            at = h * 64 + j * 16
+            field_columns[:, at : at + 16, :] = moved_fields[:, h]
+    for p in range(4):
+        field_cells[p] = field_columns[p].astype(F32).T.astype(BF)
+    for mm in range(2):
+        parts = []
+        for h in range(2):
+            total = None
+            for i in range(3):
+                rows = field_cells[2 * mm : 2 * mm + 2, i * 16 : i * 16 + 256, :]
+                term = dot(rows.reshape(512, 128), field_weights[h, i])
+                total = term if total is None else total + term
+            parts.append(total.reshape(2, 256, 256))
+        for k in range(4):
+            rows = slice(k * 16, k * 16 + 16)
             add = dot_t(back_in[mm, rows, 0:256], back[...])
-            tile = (first[mm, k].astype(F32) + add).astype(BF)
-            result[mm, k] = tile
-            extra = dot_t(back_in[mm, rows, 256:384], back[...])
-            strips = [
-                (air_second[3](mm, k * 4 + s).astype(F32) + extra[s * 16 : s * 16 + 16]).astype(BF)
-                for s in range(4)
-            ]
-            stage_tile(k, tile, strips, pad_a, shifted)
-
-        result[mm] = (result[mm].astype(F32).reshape(1024, 256)
-                      + convolve(shifted, filt_b, bias_b)).astype(BF).reshape(4, 256, 256)
+            tile = (first[mm, k].astype(F32) + add).astype(BF).astype(F32)
+            total = sums[mm, k * 256 : k * 256 + 256] + parts[k % 2][k // 2] + bias_b[...]
+            result[mm, k] = (tile + gelu(total)).astype(BF)
 
     for copy in own_copies + [onward_right, onward_left] + twin_copies:
         copy.wait_send()
     for d in range(1, 8):
         sea_copy(d).wait_send()
         flux_copy(d).wait_send()
-        skin_copy(d).wait_send()
+        skin_copy(d, 0).wait_send()
+        skin_copy(d, 1).wait_send()
     for k in range(2):
         unless_me(k, lambda: first_flux(k).wait_send())
         unless_me(k, lambda: last_skin(k).wait_send())
@@ -684,7 +728,7 @@
             jax.ShapeDtypeStruct((16, 256, 256), BF),
         ),
         in_specs=[VMEM] * 3 + [HBM, VMEM, HBM] + [VMEM] * 6 + [HBM, VMEM, HBM] + [VMEM] * 11
-        + [HBM, VMEM] + [SMEM] * 4,
+        + [HBM, VMEM, VMEM] + [SMEM] * 4,
         out_specs=(VMEM, VMEM),
         scratch_shapes=[
             pltpu.VMEM((9, 256, 256), BF),
@@ -724,11 +768,15 @@
             pltpu.VMEM((16, 384, 256), BF),
             pltpu.VMEM((128, 256), BF),
             pltpu.VMEM((128, 1024), BF),
+            pltpu.VMEM((2, 1024, 256), F32),
+            pltpu.VMEM((2, 3, 128, 256), BF),
+            pltpu.VMEM((4, 128, 384), BF),
+            pltpu.VMEM((4, 384, 128), BF),
             dma((2, 2, 2, 3)), dma((2, 2, 2, 3)),
             dma((11,)), dma((11,)),
             dma((7,)), dma((7,)),
             dma((9,)), dma((9,)),
-            dma((9,)), dma((9,)),
+            dma((16,)), dma((16,)),
         ],
         compiler_params=pltpu.CompilerParams(
             collective_id=0, has_side_effects=True, vmem_limit_bytes=60 * 1024 * 1024),

time: 114 us -> 102 us (0.89)
  Pallas kernels: 108 us -> 95.7 us
    pallas_call x1, Pallas kernels: 108 us -> 95.7 us  [on_device(): pl.pallas_call(kernel, out_shape=(jax.ShapeDtypeStruct((2, 4, 256, 256),...]
where the time goes in v4:
time: 102 us; the launch traced here: 101 us
  Pallas kernels  95.7 us (94%)
  local copies, waits for them, and re-layouts  3.73 us (4%)
  other arithmetic  1.29 us (1%)
    pallas_call x1, Pallas kernels, on_device(): pl.pallas_call(kernel, out_shape=(jax.ShapeDtypeStruct((2, 4, 256, 256),...  95.7 us
    unnamed x4, local copies, waits for them, and re-layouts  3.73 us

profile of v4, /device:TPU:25, one launch (start us, length us, event | category | flops | bytes accessed | tf_op | source)
XLA Modules:
  0.0 101.4 jit_solution(9660265421075485569)
XLA Ops:
  0.6 0.7 broadcast_shift-right-arithmetic_fusion
  1.3 0.6 select_reduce_fusion.places
  1.9 95.7 %shard_map.311 = (bf16[2,4,256,256]{3,2,1,0:T(8,128)(2,1)}, bf16[16,256,256]{2,1,0:T(8,128)(2,1)}) custom-call(bf16[2,4,256,256]{3,2,1,0:T(8,128)(2,1)} %air.1, bf16[16,256,256]{2,1,0:T(8,128)(2,1)} %bitcast.12, s32[16,256]{1,0:T(8,128)} %sea.1, bf16[9,256,256]{2,1,0:T(8,128)(2,1)} %filt_a_far.1, f32[1,256]{1,0:T(1,128)} %bitcast.18, ...), custom_call_target="tpu_custom_call" | custom-call | tf_op jit(solution)/shard_map/pallas_call | solution.py:724
  97.7 0.0 copy-start
  97.7 2.4 %copy.36 = bf16[2,4,256,256]{3,2,1,0:T(8,128)(2,1)} copy(bf16[2,4,256,256]{3,2,1,0:T(8,128)(2,1)} %get-tuple-element.10) | data formatting | bytes 2097152
  100.1 0.0 copy-done
  100.1 1.3 %copy.37 = bf16[1,16,256,256]{3,2,1,0:T(8,128)(2,1)} copy(bf16[1,16,256,256]{3,2,1,0:T(8,128)(2,1)S(1)} %bitcast.11) | data formatting | bytes 4194304
Async XLA Ops:
  97.7 2.4 %copy-start = (bf16[16,256,256]{2,1,0:T(8,128)(2,1)S(1)}, bf16[16,256,256]{2,1,0:T(8,128)(2,1)}, u32[]{:S(2)}) copy-start(bf16[16,256,256]{2,1,0:T(8,128)(2,1)} %get-tuple-element.5) | copy-start | bytes 6291460

commit v5 on v4

--- a/solution.py
+++ b/solution.py
@@ -296,12 +296,12 @@
     return [value.reshape(16, 256) for value in total]
 
 
-def kernel(air, marine, sea, filt_a_far, bias_a, filt_b_far, bias_b, flux_t, exchange, wide_in,
+def kernel(air_far, marine_far, sea, filt_a_far, bias_a, filt_b_far, bias_b, flux_t, exchange, wide_in,
            wide_bias, gain, entry_far, entry_bias, leave_far, skin_t, back,
-           split, join, air_rim, ocean_rim, side_sel, strip_sel, up, up_rim, pick, shift_far, shift_air, mean,
+           split, join, air_rim, ocean_rim, side_sel, strip_far, up, up_rim_far, pick_far, shift_far, shift_air_far, mean,
            air_nbr, ocean_nbr, quarter, places,
            result, advanced,
-           filt_a, filt_b, entry, leave, shift, fetch,
+           filt_a, filt_b, entry, leave, shift, air, marine, strip_sel, up_rim, pick, shift_air, fetch,
            first, pad_a, shifted, g00, g01, g10, g11, st, r00, r01, r10, r11,
            rims, sea_all, wet32, flux_own, flux_in, skin_in, back_out, back_in,
            wide, weights, pad_o, moved, pad_r, depth, normed_even, normed_odd, fine_flux,
@@ -367,15 +367,18 @@
         pltpu.make_async_copy(far, near, fetch.at[n])
         for n, (far, near) in enumerate((
             (filt_a_far, filt_a), (shift_far, shift), (entry_far, entry), (leave_far, leave),
-            (filt_b_far, filt_b)))
+            (filt_b_far, filt_b), (air_far, air), (marine_far, marine), (strip_far, strip_sel),
+            (up_rim_far, up_rim), (pick_far, pick), (shift_air_far, shift_air)))
     ]
-    for copy in fetches:
-        copy.start()
+    for n in (5, 6, 0, 1, 2, 3, 4, 7, 8, 9, 10):
+        fetches[n].start()
+    fetches[5].wait()
     air_first = rim_exchange(0, air, air_nbr, air_rim, g1, st, r2, asend, arecv)
     air_second = rim_exchange(1, first, air_nbr, air_rim, g1, st, r2, asend, arecv)
     air_first[0](0)
     air_first[0](1)
     sea_all[o] = sea[...].astype(F32).astype(BF)
+    fetches[6].wait()
 
     @pl.loop(0, 16, unroll=4)
     def _(t):
@@ -410,6 +413,8 @@
             interior(tile, wide, wide_bias, pad_o, moved, depth.at[t])
 
     interiors(0, 5)
+    for n in (7, 8, 9, 10):
+        fetches[n].wait()
     air_first[1]()
     interiors(5, 11)
     air_first[2]()
@@ -522,14 +527,7 @@
 
         sums[mm] = convolve(shifted, filt_b)
 
-    air_second[2]()
     fetches[4].wait()
-    early_sums(0)
-
-    onward_right.wait_recv()
-    twin_copies[3].start()
-    onward_left.wait_recv()
-    twin_copies[4].start()
     field_weights[...] = jnp.zeros(field_weights.shape, BF)
     for h in range(2):
         for i in range(3):
@@ -537,12 +535,16 @@
                 at = h * 64 + j * 16
                 field_weights[h, i, at : at + 16] = dot(back[...], filt_b[3 * i + j]).astype(BF)
     field_columns[...] = jnp.zeros(field_columns.shape, BF)
-    for copy in twin_copies:
-        copy.wait_recv()
-
+
+    onward_right.wait_recv()
+    twin_copies[3].start()
+    onward_left.wait_recv()
+    twin_copies[4].start()
     fetches[2].wait()
     fetches[3].wait()
     leave[...] = (leave[...].astype(F32) * 0.5).astype(BF)
+    for copy in twin_copies:
+        copy.wait_recv()
 
     def add_rim(t, h, s):
         n = ocean_nbr[s, o * 16 + t]
@@ -614,7 +616,8 @@
 
     for d in range(1, 8):
         skin_copy(d, 1).start()
-    early_sums(1)
+    air_second[2]()
+    early_sums(0)
 
     for d in range(1, 8):
         skin_copy(d, 0).wait_recv()
@@ -628,7 +631,7 @@
         inside = jnp.where(lane < 64, 0, 1) == b
         return jnp.where(inside, turned, 0.0).astype(BF)
 
-    @pl.loop(0, 8)
+    @pl.loop(0, 8, unroll=4)
     def _(k):
         rows = pl.ds(pl.multiple_of(k * 16, 16), 16)
         tile = o * 8 + k
@@ -650,6 +653,7 @@
         def _():
             back_in[k] = back_out[k]
 
+    early_sums(1)
     for mm in range(2):
         def arrival():
             remote(back_out.at[0], back_in.at[mm], ksend.at[mm], krecv.at[mm],
@@ -717,7 +721,8 @@
     index = lax.broadcasted_iota(jnp.int32, (128, 128), 0)
     tile = lax.broadcasted_iota(jnp.int32, (128, 128), 1)
     covered = jnp.broadcast_to(marine_spanned_quarter[None, :], (128, 128))
-    code = jnp.where((covered >> 1) == index, 2 * tile + (covered & 1), 0)
+    code = jnp.where(covered == 2 * index, 2 * tile, 0)
+    code = jnp.where(covered == 2 * index + 1, 2 * tile + 1, code)
     places = jnp.sum(code, axis=1)
     strips = pltpu.VMEM((4, 16, 16, 256), BF)
     dma = pltpu.SemaphoreType.DMA
@@ -727,8 +732,8 @@
             jax.ShapeDtypeStruct((2, 4, 256, 256), BF),
             jax.ShapeDtypeStruct((16, 256, 256), BF),
         ),
-        in_specs=[VMEM] * 3 + [HBM, VMEM, HBM] + [VMEM] * 6 + [HBM, VMEM, HBM] + [VMEM] * 11
-        + [HBM, VMEM, VMEM] + [SMEM] * 4,
+        in_specs=[HBM, HBM, VMEM, HBM, VMEM, HBM] + [VMEM] * 6 + [HBM, VMEM, HBM] + [VMEM] * 7
+        + [HBM, VMEM] + [HBM] * 4 + [VMEM] + [SMEM] * 4,
         out_specs=(VMEM, VMEM),
         scratch_shapes=[
             pltpu.VMEM((9, 256, 256), BF),
@@ -736,7 +741,13 @@
             pltpu.VMEM((256, 1024), BF),
             pltpu.VMEM((1024, 256), BF),
             pltpu.VMEM((512, 2688), BF),
-            dma((5,)),
+            pltpu.VMEM((2, 4, 256, 256), BF),
+            pltpu.VMEM((16, 256, 256), BF),
+            pltpu.VMEM((1024, 128), BF),
+            pltpu.VMEM((512, 256), BF),
+            pltpu.VMEM((1024, 256), BF),
+            pltpu.VMEM((384, 1152), BF),
+            dma((11,)),
             pltpu.VMEM((2, 4, 256, 256), BF),
             pltpu.VMEM((18, 32, 256), F32),
             pltpu.VMEM((3, 4, 288, 256), BF),

time: 102 us -> 101 us (level)
  no operation moved by 1% of the time
where the time goes in v5:
time: 101 us
  Pallas kernels  95.2 us (94%)
  local copies, waits for them, and re-layouts  3.73 us (4%)
  other arithmetic  1.36 us (1%)
    pallas_call x1, Pallas kernels, on_device(): pl.pallas_call(kernel, out_shape=(jax.ShapeDtypeStruct((2, 4, 256, 256),...  95.2 us
    unnamed x4, local copies, waits for them, and re-layouts  3.73 us

profile of v5, /device:TPU:25, one launch (start us, length us, event | category | flops | bytes accessed | tf_op | source)
XLA Modules:
  0.0 101.0 jit_solution(9022624770382521206)
XLA Ops:
  0.6 1.4 %select_reduce_fusion.places = s32[128]{0:T(128)} fusion(s32[128]{0:T(128)S(1)} %get-tuple-element.6, s32[128]{0:T(128)S(1)} %get-tuple-element.7, s32[128]{0:T(128)} %quarter.1), kind=kLoop, calls=%fused_computation | loop fusion | flops 81792 | bytes 2048 | tf_op jit(solution)/shard_map/reduce_sum | solution.py:726
  2.0 95.2 %shard_map.311 = (bf16[2,4,256,256]{3,2,1,0:T(8,128)(2,1)}, bf16[16,256,256]{2,1,0:T(8,128)(2,1)}) custom-call(bf16[2,4,256,256]{3,2,1,0:T(8,128)(2,1)} %air_far.1, bf16[16,256,256]{2,1,0:T(8,128)(2,1)} %bitcast.12, s32[16,256]{1,0:T(8,128)} %sea.1, bf16[9,256,256]{2,1,0:T(8,128)(2,1)} %filt_a_far.1, f32[1,256]{1,0:T(1,128)} %bitcast.18, ...), custom_call_target="tpu_custom_call" | custom-call | tf_op jit(solution)/shard_map/pallas_call | solution.py:729
  97.2 0.0 copy-start
  97.2 2.4 %copy.36 = bf16[2,4,256,256]{3,2,1,0:T(8,128)(2,1)} copy(bf16[2,4,256,256]{3,2,1,0:T(8,128)(2,1)} %get-tuple-element.10) | data formatting | bytes 2097152
  99.6 0.0 copy-done
  99.6 1.3 %copy.37 = bf16[1,16,256,256]{3,2,1,0:T(8,128)(2,1)} copy(bf16[1,16,256,256]{3,2,1,0:T(8,128)(2,1)S(1)} %bitcast.11) | data formatting | bytes 4194304
  (1 shorter events, 0.0 us)
Async XLA Ops:
  97.2 2.4 %copy-start = (bf16[16,256,256]{2,1,0:T(8,128)(2,1)S(1)}, bf16[16,256,256]{2,1,0:T(8,128)(2,1)}, u32[]{:S(2)}) copy-start(bf16[16,256,256]{2,1,0:T(8,128)(2,1)} %get-tuple-element.5) | copy-start | bytes 6291460
